TPU v7x, 512 devices: a whole 4x4x16 slice. The times are simulated.
512 devices in a mesh: slab: 16 (over x_lo, y, core), coef: 32 (over x_hi, z).
Axes of the slice: x: 4 (x_hi: 2, x_lo: 2; x = x_hi * 2 + x_lo), y: 4, z: 16, core: 2. Of those that a mesh axis runs over, the one named last changes fastest.
Arguments:
- cotangent: float32 [8192, 4096], P('slab', 'coef'), may hold values from -6 to 6
- transport_state: bfloat16 [8192, 4096], P('slab', 'coef'), may hold values from -6 to 6
- source_state: bfloat16 [8192, 4096], P('slab', 'coef'), may hold values from -6 to 6
- courant: float32 [8192], P('slab'), may hold values from 0.2 to 1.2
- upwind_codes: int32 [8192], P('slab'), may hold values from 0 to 1
- strain_rate: float32 [9, 8192], P(None, ('slab', 'coef')), may hold values from -4 to 4
Outputs:
- adj_source: float32 [8192, 4096], P('slab', 'coef')
- adj_strain: float32 [9, 8192], P(None, ('slab', 'coef'))
- adj_courant: float32 [8192], P(('slab', 'coef'))
All inputs are finite; a program needn't handle non-finite values.
Results may differ from a plain program's by a relative error of at most 0.0003.
Values may be sent and summed in bfloat16 or wider, within the bound.
A program may use at most 64 MiB of HBM per device.

v0:
```python
import math

import jax
import jax.numpy as jnp
from jax import lax
from jax.sharding import PartitionSpec as P

CYZ = 128
NH = 16
QP = 24
K = 4096


section_weights = (0.25, 1.0 / 3.0, 0.5, 1.0)
quad_half = 4.5
fene_limit = 64.0
time_step = 0.005
highest = lax.Precision.HIGHEST
pair_rows = (0, 1, 2, 4, 5, 8)
pair_slots = (0, 1, 2, 1, 3, 4, 2, 4, 5)


def extended(block, sides, width):
    for axis, dim in sides:
        count = lax.axis_size(axis)
        forward = [(i, i + 1) for i in range(count - 1)]
        forward.append((count - 1, 0))
        backward = [(target, source) for source, target in forward]
        low = lax.ppermute(
            lax.slice_in_dim(block, block.shape[dim] - width, None, axis=dim), axis, forward
        )
        high = lax.ppermute(lax.slice_in_dim(block, 0, width, axis=dim), axis, backward)
        block = jnp.concatenate([low, block, high], axis=dim)
    return block


def shifted(shard, axis, by):
    count = lax.axis_size(axis)
    return lax.ppermute(shard, axis, [(i, (i + by) % count) for i in range(count)])


def hermite_table(mode_count, points):
    node_list = quad_half * (2.0 * jnp.arange(points, dtype=jnp.float32) + 1.0 - points) / points
    leading = jnp.exp(-0.5 * node_list * node_list) * math.pi ** (-0.25)
    table_rows = [leading, math.sqrt(2.0) * node_list * leading]
    for degree in range(1, mode_count - 1):
        table_rows.append(
            math.sqrt(2.0 / (degree + 1.0)) * node_list * table_rows[degree]
            - math.sqrt(degree / (degree + 1.0)) * table_rows[degree - 1]
        )
    return (jnp.stack(table_rows[:mode_count]), node_list)


def quadrature_tables(mode_count, points):
    hermite, node_list = hermite_table(mode_count, points)
    cube_shape = (points, points, points)
    coords = (
        jnp.broadcast_to(node_list[:, None, None], cube_shape).reshape(-1),
        jnp.broadcast_to(node_list[None, :, None], cube_shape).reshape(-1),
        jnp.broadcast_to(node_list[None, None, :], cube_shape).reshape(-1),
    )
    spring = (
        1.0 - (coords[0] * coords[0] + coords[1] * coords[1] + coords[2] * coords[2]) / fene_limit
    )
    pair_table = jnp.stack(
        [
            coords[left_dim] * coords[right_dim] / spring
            for left_dim in range(3)
            for right_dim in range(3)
        ]
    )
    return (hermite, pair_table)


def joined_values(coeffs, hermite, kron_table):
    cell_count = coeffs.shape[0]
    mode_count, points = hermite.shape
    inner_part = jnp.dot(
        coeffs.reshape(cell_count * mode_count, mode_count * mode_count),
        kron_table,
        preferred_element_type=jnp.float32,
        precision=highest,
    )
    outer_part = jnp.einsum(
        "cim,ia->cam",
        inner_part.reshape(cell_count, mode_count, points * points),
        hermite,
        precision=highest,
    )
    return outer_part.reshape(cell_count, points**3)


def joined_coefficients(values, hermite, kron_table):
    cell_count = values.shape[0]
    mode_count, points = hermite.shape
    inner_part = jnp.einsum(
        "cam,ia->cim",
        values.reshape(cell_count, points, points * points),
        hermite,
        precision=highest,
    )
    outer_part = jnp.dot(
        inner_part.reshape(cell_count * mode_count, points * points),
        kron_table.T,
        preferred_element_type=jnp.float32,
        precision=highest,
    )
    return outer_part.reshape(cell_count, mode_count**3)


def body(cotangent, transport_state, source_state, courant, upwind_codes, strain_rate):
    row_count, coef_width = cotangent.shape
    plane_count = row_count // CYZ
    grid_shape = (plane_count, CYZ, coef_width)
    speed_grid = courant.reshape(plane_count, CYZ, 1)
    upper_mask = (upwind_codes == 1).astype(jnp.float32).reshape(plane_count, CYZ, 1)
    lower_mask = 1.0 - upper_mask
    initial = transport_state.astype(jnp.float32).reshape(grid_shape)
    differences = []
    section_now = initial
    for section_no in range(4):
        padded = extended(section_now, (("slab", 0),), 1)
        change = lower_mask * (section_now - padded[:-2]) + upper_mask * (padded[2:] - section_now)
        differences.append(change)
        if section_no < 3:
            section_now = initial - section_weights[section_no] * speed_grid * change
    adjoint = cotangent.reshape(grid_shape)
    accumulated = jnp.zeros(grid_shape, jnp.float32)
    speed_part = jnp.zeros((plane_count, CYZ), jnp.float32)
    for section_no in (3, 2, 1, 0):
        speed_part = speed_part - section_weights[section_no] * jnp.sum(
            adjoint * differences[section_no], axis=2
        )
        accumulated = accumulated + adjoint
        weighted = speed_grid * adjoint
        low_part = lower_mask * weighted
        high_part = upper_mask * weighted
        from_above = shifted(low_part[:1], "slab", -1)
        from_below = shifted(high_part[-1:], "slab", 1)
        next_low = jnp.concatenate([low_part[1:], from_above], axis=0)
        prior_high = jnp.concatenate([from_below, high_part[:-1]], axis=0)
        adjoint = -section_weights[section_no] * (low_part - next_low - high_part + prior_high)
    mu_field = (accumulated + adjoint).reshape(row_count, coef_width)
    speed_column = speed_part.reshape(row_count, 1)
    mu_cells, speed_columns = (
        lax.all_to_all(mu_field, "coef", split_axis=0, concat_axis=1, tiled=True),
        lax.all_to_all(speed_column, "coef", split_axis=0, concat_axis=1, tiled=True),
    )
    source_cells = lax.all_to_all(source_state, "coef", split_axis=0, concat_axis=1, tiled=True)
    source_wide = source_cells.astype(jnp.float32)
    adj_courant = jnp.sum(speed_columns, axis=1) / math.sqrt(K)
    hermite, pair_table = quadrature_tables(NH, QP)
    kron_table = (hermite[:, None, :, None] * hermite[None, :, None, :]).reshape(NH * NH, QP * QP)
    weight_cube = (2.0 * quad_half / QP) ** 3
    adj_values = weight_cube * joined_values(mu_cells, hermite, kron_table)
    multiplier = 1.0 + time_step * jnp.einsum(
        "sc,sq->cq", strain_rate, pair_table, precision=highest
    )
    adj_cells = joined_coefficients(multiplier * adj_values, hermite, kron_table)
    unique_table = jnp.stack([pair_table[slot_no] for slot_no in pair_rows])
    source_values = joined_values(source_wide, hermite, kron_table)
    strain_unique = time_step * jnp.einsum(
        "pq,cq->pc", unique_table, adj_values * source_values, precision=highest
    )
    adj_source = lax.all_to_all(adj_cells, "coef", split_axis=1, concat_axis=0, tiled=True)
    adj_strain = jnp.stack([strain_unique[slot_no] for slot_no in pair_slots])
    return (adj_source, adj_strain, adj_courant)


def solution(mesh):
    placed = (
        P("slab", "coef"),
        P("slab", "coef"),
        P("slab", "coef"),
        P("slab"),
        P("slab"),
        P(None, ("slab", "coef")),
    )
    return jax.shard_map(
        body,
        mesh=mesh,
        in_specs=placed,
        out_specs=(P("slab", "coef"), P(None, ("slab", "coef")), P(("slab", "coef"))),
        check_vma=False,
    )
```

profile of v0, /device:TPU:24, one launch (start us, length us, event | category | flops | bytes accessed | tf_op | source)
XLA Modules:
  0.0 190.6 jit_solution(3589017161790618663)
XLA Ops:
  1.7 2.1 %collective-permute-start.9 = (f32[1,128,128]{2,1,0:T(8,128)S(1)}, f32[1,128,128]{2,1,0:T(8,128)S(1)}, u32[]{:S(2)}, u32[]{:S(2)}) collective-permute-start(f32[1,128,128]{2,1,0:T(8,128)S(1)} %get-tuple-element.28), channel_id=1, source_target_pairs={{32,0},{64,32},{96,64},{128,96},{160,128},{192,160},{224,192},{256... | collective-permute-start | bytes 196616 | tf_op jit(solution)/shard_map/ppermute | solution.py:32
  3.8 2.2 %collective-permute-start.8 = (f32[1,128,128]{2,1,0:T(8,128)S(1)}, f32[1,128,128]{2,1,0:T(8,128)S(1)}, u32[]{:S(2)}, u32[]{:S(2)}) collective-permute-start(f32[1,128,128]{2,1,0:T(8,128)S(1)} %get-tuple-element.27), channel_id=1, source_target_pairs={{0,32},{32,64},{64,96},{96,128},{128,160},{160,192},{192,224},{224... | collective-permute-start | bytes 196616 | tf_op jit(solution)/shard_map/ppermute | solution.py:29
  11.1 3.3 %collective-permute-start.11 = (f32[1,128,128]{2,1,0:T(8,128)S(1)}, f32[1,128,128]{2,1,0:T(8,128)S(1)}, u32[]{:S(2)}, u32[]{:S(2)}) collective-permute-start(f32[1,128,128]{2,1,0:T(8,128)S(1)} %get-tuple-element.26), channel_id=1, source_target_pairs={{32,0},{64,32},{96,64},{128,96},{160,128},{192,160},{224,192},{256... | collective-permute-start | bytes 196616 | tf_op jit(solution)/shard_map/ppermute | solution.py:32
  14.4 3.7 %collective-permute-start.10 = (f32[1,128,128]{2,1,0:T(8,128)S(1)}, f32[1,128,128]{2,1,0:T(8,128)S(1)}, u32[]{:S(2)}, u32[]{:S(2)}) collective-permute-start(f32[1,128,128]{2,1,0:T(8,128)S(1)} %get-tuple-element.25), channel_id=1, source_target_pairs={{0,32},{32,64},{64,96},{96,128},{128,160},{160,192},{192,224},{224... | collective-permute-start | bytes 196616 | tf_op jit(solution)/shard_map/ppermute | solution.py:29
  22.2 5.2 %collective-permute-start.12 = (f32[1,128,128]{2,1,0:T(8,128)S(1)}, f32[1,128,128]{2,1,0:T(8,128)S(1)}, u32[]{:S(2)}, u32[]{:S(2)}) collective-permute-start(f32[1,128,128]{2,1,0:T(8,128)S(1)} %get-tuple-element.23), channel_id=1, source_target_pairs={{0,32},{32,64},{64,96},{96,128},{128,160},{160,192},{192,224},{224... | collective-permute-start | bytes 196616 | tf_op jit(solution)/shard_map/ppermute | solution.py:29
  28.7 6.8 %collective-permute-start.1 = (f32[1,128,128]{2,1,0:T(8,128)S(1)}, f32[1,128,128]{2,1,0:T(8,128)S(1)}, u32[]{:S(2)}, u32[]{:S(2)}) collective-permute-start(f32[1,128,128]{2,1,0:T(8,128)S(1)} %slice.173), channel_id=1, source_target_pairs={{0,32},{32,64},{64,96},{96,128},{128,160},{160,192},{192,224},{224... | collective-permute-start | bytes 196616 | tf_op jit(solution)/shard_map/ppermute | solution.py:39
  39.4 6.4 %collective-permute-start.14 = (f32[1,128,128]{2,1,0:T(8,128)S(1)}, f32[1,128,128]{2,1,0:T(8,128)S(1)}, u32[]{:S(2)}, u32[]{:S(2)}) collective-permute-start(f32[1,128,128]{2,1,0:T(8,128)S(1)} %get-tuple-element.21), channel_id=1, source_target_pairs={{0,32},{32,64},{64,96},{96,128},{128,160},{160,192},{192,224},{224... | collective-permute-start | bytes 196616 | tf_op jit(solution)/shard_map/ppermute | solution.py:29
  46.3 5.8 %collective-permute-start.3 = (f32[1,128,128]{2,1,0:T(8,128)S(1)}, f32[1,128,128]{2,1,0:T(8,128)S(1)}, u32[]{:S(2)}, u32[]{:S(2)}) collective-permute-start(f32[1,128,128]{2,1,0:T(8,128)S(1)} %slice.177), channel_id=1, source_target_pairs={{0,32},{32,64},{64,96},{96,128},{128,160},{160,192},{192,224},{224... | collective-permute-start | bytes 196616 | tf_op jit(solution)/shard_map/ppermute | solution.py:39
  56.7 6.3 %collective-permute-start.5 = (f32[1,128,128]{2,1,0:T(8,128)S(1)}, f32[1,128,128]{2,1,0:T(8,128)S(1)}, u32[]{:S(2)}, u32[]{:S(2)}) collective-permute-start(f32[1,128,128]{2,1,0:T(8,128)S(1)} %slice.181), channel_id=1, source_target_pairs={{0,32},{32,64},{64,96},{96,128},{128,160},{160,192},{192,224},{224... | collective-permute-start | bytes 196616 | tf_op jit(solution)/shard_map/ppermute | solution.py:39
  63.0 1.9 %collective-permute-start.4 = (f32[1,128,128]{2,1,0:T(8,128)S(1)}, f32[1,128,128]{2,1,0:T(8,128)S(1)}, u32[]{:S(2)}, u32[]{:S(2)}) collective-permute-start(f32[1,128,128]{2,1,0:T(8,128)S(1)} %slice.180), channel_id=1, source_target_pairs={{0,480},{32,0},{64,32},{96,64},{128,96},{160,128},{192,160},{224,1... | collective-permute-start | bytes 196616 | tf_op jit(solution)/shard_map/ppermute | solution.py:39
  67.6 5.8 %collective-permute-start.7 = (f32[1,128,128]{2,1,0:T(8,128)S(1)}, f32[1,128,128]{2,1,0:T(8,128)S(1)}, u32[]{:S(2)}, u32[]{:S(2)}) collective-permute-start(f32[1,128,128]{2,1,0:T(8,128)S(1)} %slice.185), channel_id=1, source_target_pairs={{0,32},{32,64},{64,96},{96,128},{128,160},{160,192},{192,224},{224... | collective-permute-start | bytes 196616 | tf_op jit(solution)/shard_map/ppermute | solution.py:39
  73.4 1.9 %collective-permute-start.6 = (f32[1,128,128]{2,1,0:T(8,128)S(1)}, f32[1,128,128]{2,1,0:T(8,128)}, u32[]{:S(2)}, u32[]{:S(2)}) collective-permute-start(f32[1,128,128]{2,1,0:T(8,128)S(1)} %slice.184), channel_id=1, source_target_pairs={{0,480},{32,0},{64,32},{96,64},{128,96},{160,128},{192,160},{224,1... | collective-permute-start | bytes 196616 | tf_op jit(solution)/shard_map/ppermute | solution.py:39
  76.1 17.9 %all-to-all-start.3 = ((f32[32,16,1]{1,2,0:T(1,128)}), f32[32,16,1]{1,2,0:T(1,128)S(1)}, u32[]{:S(2)}, u32[]{:S(2)}) async-start(f32[32,16,1]{1,2,0:T(1,128)} %bitcast.29), calls=%async_computation.3 | async-start | bytes 32768 | tf_op jit(solution)/shard_map/all_to_all | solution.py:147
  94.1 14.7 %all-to-all-done.3 = f32[32,16,1]{1,2,0:T(1,128)S(1)} async-done(((f32[32,16,1]{1,2,0:T(1,128)}), f32[32,16,1]{1,2,0:T(1,128)S(1)}, u32[]{:S(2)}, u32[]{:S(2)}) %all-to-all-start.3) | async-done | bytes 2080 | tf_op jit(solution)/shard_map/all_to_all | solution.py:147
  108.8 3.9 %all-to-all-start.2 = ((bf16[32,16,128]{2,1,0:T(8,128)(2,1)}), bf16[32,16,128]{2,1,0:T(8,128)(2,1)S(1)}, u32[]{:S(2)}, u32[]{:S(2)}) async-start(bf16[32,16,128]{2,1,0:T(8,128)(2,1)} %bitcast.21), calls=%async_computation.2 | async-start | bytes 262144 | tf_op jit(solution)/shard_map/all_to_all | solution.py:149
  114.8 15.6 %all-to-all-done.2 = bf16[32,16,128]{2,1,0:T(8,128)(2,1)S(1)} async-done(((bf16[32,16,128]{2,1,0:T(8,128)(2,1)}), bf16[32,16,128]{2,1,0:T(8,128)(2,1)S(1)}, u32[]{:S(2)}, u32[]{:S(2)}) %all-to-all-start.2) | async-done | bytes 131104 | tf_op jit(solution)/shard_map/all_to_all | solution.py:149
  130.5 4.1 %all-to-all-start = ((f32[32,16,128]{2,1,0:T(8,128)}), f32[32,16,128]{2,1,0:T(8,128)S(1)}, u32[]{:S(2)}, u32[]{:S(2)}) async-start(f32[32,16,128]{2,1,0:T(8,128)} %bitcast.13), calls=%async_computation | async-start | bytes 524288 | tf_op jit(solution)/shard_map/all_to_all | solution.py:146
  134.6 3.6 %stack.10 = f32[9,13824]{1,0:T(8,128)} concatenate(f32[1,13824]{1,0:T(1,128)} %get-tuple-element.33, f32[1,13824]{1,0:T(1,128)S(1)} %get-tuple-element.32, f32[1,13824]{1,0:T(1,128)S(1)} %get-tuple-element.31, f32[1,13824]{1,0:T(1,128)S(1)} %get-tuple-element.32, f32[1,13824]{1,0:T(1,128)S(1)} %get-tuple-element.30, f32[1,13824]{1,0:T(1,128)S(1)} %get-tuple-element.29, ...), dimensions={0} | concatenate | bytes 995328 | tf_op jit(solution)/shard_map/stack | solution.py:65
  143.1 13.5 %all-to-all-done = f32[32,16,128]{2,1,0:T(8,128)S(1)} async-done(((f32[32,16,128]{2,1,0:T(8,128)}), f32[32,16,128]{2,1,0:T(8,128)S(1)}, u32[]{:S(2)}, u32[]{:S(2)}) %all-to-all-start) | async-done | bytes 262176 | tf_op jit(solution)/shard_map/all_to_all | solution.py:146
  159.9 2.2 %fusion.2 = f32[16,13824]{1,0:T(8,128)S(1)} fusion(f32[16,13824]{1,0:T(8,128)S(1)} %mul.3484, f32[9,13824]{1,0:T(8,128)} %stack.10, f32[9,16]{1,0:T(8,128)S(1)} %copy-done), kind=kOutput, calls=%fused_computation.3 | convolution fusion | flops 24551424 | bytes 2267712 | tf_op jit(solution)/shard_map/sc,sq->cq/dot_general | solution.py:156
  164.9 3.9 %all-to-all-start.1 = ((f32[16,32,128]{2,0,1:T(8,128)}), f32[16,32,128]{2,0,1:T(8,128)S(1)}, u32[]{:S(2)}, u32[]{:S(2)}) async-start(f32[16,32,128]{2,0,1:T(8,128)} %copy.17), calls=%async_computation.1 | async-start | bytes 524288 | tf_op jit(solution)/shard_map/all_to_all | solution.py:165
  170.9 2.2 %convolution_multiply_fusion.2 = f32[6,16]{1,0:T(8,128)S(1)} fusion(f32[6,13824]{1,0:T(8,128)} %stack.11, f32[16,13824]{1,0:T(8,128)S(1)} %mul.3484, f32[16,13824]{1,0:T(8,128)S(1)} %reshape.613), kind=kOutput, calls=%fused_computation.9 | convolution fusion | flops 16146528 | bytes 2101632 | tf_op jit(solution)/shard_map/pq,cq->pc/dot_general | solution.py:162
  173.1 2.0 %stack.12 = f32[9,16]{1,0:T(8,128)} concatenate(f32[3,16]{1,0:T(4,128)S(1)} %slice.148, f32[1,16]{1,0:T(1,128)S(1)} %get-tuple-element.38, f32[2,16]{1,0:T(2,128)S(1)} %get-tuple-element.36, f32[1,16]{1,0:T(1,128)S(1)} %get-tuple-element.37, f32[2,16]{1,0:T(2,128)S(1)} %get-tuple-element.35), dimensions={0} | concatenate | bytes 1152 | tf_op jit(solution)/shard_map/stack | solution.py:166
  175.1 14.8 %all-to-all-done.1 = f32[16,32,128]{2,0,1:T(8,128)S(1)} async-done(((f32[16,32,128]{2,0,1:T(8,128)}), f32[16,32,128]{2,0,1:T(8,128)S(1)}, u32[]{:S(2)}, u32[]{:S(2)}) %all-to-all-start.1) | async-done | bytes 262176 | tf_op jit(solution)/shard_map/all_to_all | solution.py:165
  (140 shorter events, 39.4 us)
Async XLA Ops:
  0.6 159.3 %copy-start = (f32[9,16]{1,0:T(8,128)S(1)}, f32[9,16]{1,0:T(8,128)}, u32[]{:S(2)}) copy-start(f32[9,16]{1,0:T(8,128)} %param.11) | copy-start | bytes 1732
  1.7 9.1 %collective-permute-start.9 = (f32[1,128,128]{2,1,0:T(8,128)S(1)}, f32[1,128,128]{2,1,0:T(8,128)S(1)}, u32[]{:S(2)}, u32[]{:S(2)}) collective-permute-start(f32[1,128,128]{2,1,0:T(8,128)S(1)} %get-tuple-element.28), channel_id=1, source_target_pairs={{32,0},{64,32},{96,64},{128,96},{160,128},{192,160},{224,192},{256... | collective-permute-start | bytes 196616 | tf_op jit(solution)/shard_map/ppermute | solution.py:32
  3.8 7.0 %collective-permute-start.8 = (f32[1,128,128]{2,1,0:T(8,128)S(1)}, f32[1,128,128]{2,1,0:T(8,128)S(1)}, u32[]{:S(2)}, u32[]{:S(2)}) collective-permute-start(f32[1,128,128]{2,1,0:T(8,128)S(1)} %get-tuple-element.27), channel_id=1, source_target_pairs={{0,32},{32,64},{64,96},{96,128},{128,160},{160,192},{192,224},{224... | collective-permute-start | bytes 196616 | tf_op jit(solution)/shard_map/ppermute | solution.py:29
  11.1 7.6 %collective-permute-start.11 = (f32[1,128,128]{2,1,0:T(8,128)S(1)}, f32[1,128,128]{2,1,0:T(8,128)S(1)}, u32[]{:S(2)}, u32[]{:S(2)}) collective-permute-start(f32[1,128,128]{2,1,0:T(8,128)S(1)} %get-tuple-element.26), channel_id=1, source_target_pairs={{32,0},{64,32},{96,64},{128,96},{160,128},{192,160},{224,192},{256... | collective-permute-start | bytes 196616 | tf_op jit(solution)/shard_map/ppermute | solution.py:32
  14.4 5.6 %collective-permute-start.10 = (f32[1,128,128]{2,1,0:T(8,128)S(1)}, f32[1,128,128]{2,1,0:T(8,128)S(1)}, u32[]{:S(2)}, u32[]{:S(2)}) collective-permute-start(f32[1,128,128]{2,1,0:T(8,128)S(1)} %get-tuple-element.25), channel_id=1, source_target_pairs={{0,32},{32,64},{64,96},{96,128},{128,160},{160,192},{192,224},{224... | collective-permute-start | bytes 196616 | tf_op jit(solution)/shard_map/ppermute | solution.py:29
  20.3 7.7 %collective-permute-start.13 = (f32[1,128,128]{2,1,0:T(8,128)S(1)}, f32[1,128,128]{2,1,0:T(8,128)S(1)}, u32[]{:S(2)}, u32[]{:S(2)}) collective-permute-start(f32[1,128,128]{2,1,0:T(8,128)S(1)} %get-tuple-element.24), channel_id=1, source_target_pairs={{32,0},{64,32},{96,64},{128,96},{160,128},{192,160},{224,192},{256... | collective-permute-start | bytes 196616 | tf_op jit(solution)/shard_map/ppermute | solution.py:32
  22.2 6.1 %collective-permute-start.12 = (f32[1,128,128]{2,1,0:T(8,128)S(1)}, f32[1,128,128]{2,1,0:T(8,128)S(1)}, u32[]{:S(2)}, u32[]{:S(2)}) collective-permute-start(f32[1,128,128]{2,1,0:T(8,128)S(1)} %get-tuple-element.23), channel_id=1, source_target_pairs={{0,32},{32,64},{64,96},{96,128},{128,160},{160,192},{192,224},{224... | collective-permute-start | bytes 196616 | tf_op jit(solution)/shard_map/ppermute | solution.py:29
  28.7 17.1 %collective-permute-start.1 = (f32[1,128,128]{2,1,0:T(8,128)S(1)}, f32[1,128,128]{2,1,0:T(8,128)S(1)}, u32[]{:S(2)}, u32[]{:S(2)}) collective-permute-start(f32[1,128,128]{2,1,0:T(8,128)S(1)} %slice.173), channel_id=1, source_target_pairs={{0,32},{32,64},{64,96},{96,128},{128,160},{160,192},{192,224},{224... | collective-permute-start | bytes 196616 | tf_op jit(solution)/shard_map/ppermute | solution.py:39
  35.5 10.3 %collective-permute-start = (f32[1,128,128]{2,1,0:T(8,128)S(1)}, f32[1,128,128]{2,1,0:T(8,128)S(1)}, u32[]{:S(2)}, u32[]{:S(2)}) collective-permute-start(f32[1,128,128]{2,1,0:T(8,128)S(1)} %slice.172), channel_id=1, source_target_pairs={{0,480},{32,0},{64,32},{96,64},{128,96},{160,128},{192,160},{224,1... | collective-permute-start | bytes 196616 | tf_op jit(solution)/shard_map/ppermute | solution.py:39
  37.5 17.1 %collective-permute-start.15 = (f32[1,128,128]{2,1,0:T(8,128)S(1)}, f32[1,128,128]{2,1,0:T(8,128)S(1)}, u32[]{:S(2)}, u32[]{:S(2)}) collective-permute-start(f32[1,128,128]{2,1,0:T(8,128)S(1)} %get-tuple-element.22), channel_id=1, source_target_pairs={{32,0},{64,32},{96,64},{128,96},{160,128},{192,160},{224,192},{256... | collective-permute-start | bytes 196616 | tf_op jit(solution)/shard_map/ppermute | solution.py:32
  39.4 15.2 %collective-permute-start.14 = (f32[1,128,128]{2,1,0:T(8,128)S(1)}, f32[1,128,128]{2,1,0:T(8,128)S(1)}, u32[]{:S(2)}, u32[]{:S(2)}) collective-permute-start(f32[1,128,128]{2,1,0:T(8,128)S(1)} %get-tuple-element.21), channel_id=1, source_target_pairs={{0,32},{32,64},{64,96},{96,128},{128,160},{160,192},{192,224},{224... | collective-permute-start | bytes 196616 | tf_op jit(solution)/shard_map/ppermute | solution.py:29
  46.3 8.4 %collective-permute-start.3 = (f32[1,128,128]{2,1,0:T(8,128)S(1)}, f32[1,128,128]{2,1,0:T(8,128)S(1)}, u32[]{:S(2)}, u32[]{:S(2)}) collective-permute-start(f32[1,128,128]{2,1,0:T(8,128)S(1)} %slice.177), channel_id=1, source_target_pairs={{0,32},{32,64},{64,96},{96,128},{128,160},{160,192},{192,224},{224... | collective-permute-start | bytes 196616 | tf_op jit(solution)/shard_map/ppermute | solution.py:39
  52.0 3.8 %collective-permute-start.2 = (f32[1,128,128]{2,1,0:T(8,128)S(1)}, f32[1,128,128]{2,1,0:T(8,128)S(1)}, u32[]{:S(2)}, u32[]{:S(2)}) collective-permute-start(f32[1,128,128]{2,1,0:T(8,128)S(1)} %slice.176), channel_id=1, source_target_pairs={{0,480},{32,0},{64,32},{96,64},{128,96},{160,128},{192,160},{224,1... | collective-permute-start | bytes 196616 | tf_op jit(solution)/shard_map/ppermute | solution.py:39
  56.7 8.3 %collective-permute-start.5 = (f32[1,128,128]{2,1,0:T(8,128)S(1)}, f32[1,128,128]{2,1,0:T(8,128)S(1)}, u32[]{:S(2)}, u32[]{:S(2)}) collective-permute-start(f32[1,128,128]{2,1,0:T(8,128)S(1)} %slice.181), channel_id=1, source_target_pairs={{0,32},{32,64},{64,96},{96,128},{128,160},{160,192},{192,224},{224... | collective-permute-start | bytes 196616 | tf_op jit(solution)/shard_map/ppermute | solution.py:39
  63.0 3.8 %collective-permute-start.4 = (f32[1,128,128]{2,1,0:T(8,128)S(1)}, f32[1,128,128]{2,1,0:T(8,128)S(1)}, u32[]{:S(2)}, u32[]{:S(2)}) collective-permute-start(f32[1,128,128]{2,1,0:T(8,128)S(1)} %slice.180), channel_id=1, source_target_pairs={{0,480},{32,0},{64,32},{96,64},{128,96},{160,128},{192,160},{224,1... | collective-permute-start | bytes 196616 | tf_op jit(solution)/shard_map/ppermute | solution.py:39
  67.6 45.1 %collective-permute-start.7 = (f32[1,128,128]{2,1,0:T(8,128)S(1)}, f32[1,128,128]{2,1,0:T(8,128)S(1)}, u32[]{:S(2)}, u32[]{:S(2)}) collective-permute-start(f32[1,128,128]{2,1,0:T(8,128)S(1)} %slice.185), channel_id=1, source_target_pairs={{0,32},{32,64},{64,96},{96,128},{128,160},{160,192},{192,224},{224... | collective-permute-start | bytes 196616 | tf_op jit(solution)/shard_map/ppermute | solution.py:39
  73.4 39.3 %collective-permute-start.6 = (f32[1,128,128]{2,1,0:T(8,128)S(1)}, f32[1,128,128]{2,1,0:T(8,128)}, u32[]{:S(2)}, u32[]{:S(2)}) collective-permute-start(f32[1,128,128]{2,1,0:T(8,128)S(1)} %slice.184), channel_id=1, source_target_pairs={{0,480},{32,0},{64,32},{96,64},{128,96},{160,128},{192,160},{224,1... | collective-permute-start | bytes 196616 | tf_op jit(solution)/shard_map/ppermute | solution.py:39
  76.1 32.7 %all-to-all-start.3 = ((f32[32,16,1]{1,2,0:T(1,128)}), f32[32,16,1]{1,2,0:T(1,128)S(1)}, u32[]{:S(2)}, u32[]{:S(2)}) async-start(f32[32,16,1]{1,2,0:T(1,128)} %bitcast.29), calls=%async_computation.3 | async-start | bytes 32768 | tf_op jit(solution)/shard_map/all_to_all | solution.py:147
  94.1 44.1 %copy-start.4 = (f32[1,13824]{1,0:T(1,128)S(1)}, f32[1,13824]{1,0:T(1,128)}, u32[]{:S(2)}) copy-start(f32[1,13824]{1,0:T(1,128)} %get-tuple-element.33) | copy-start | bytes 165892
  94.1 44.1 %copy-start.5 = (f32[1,13824]{1,0:T(1,128)S(1)}, f32[1,13824]{1,0:T(1,128)}, u32[]{:S(2)}) copy-start(f32[1,13824]{1,0:T(1,128)} %get-tuple-element.9) | copy-start | bytes 165892
  108.8 21.7 %all-to-all-start.2 = ((bf16[32,16,128]{2,1,0:T(8,128)(2,1)}), bf16[32,16,128]{2,1,0:T(8,128)(2,1)S(1)}, u32[]{:S(2)}, u32[]{:S(2)}) async-start(bf16[32,16,128]{2,1,0:T(8,128)(2,1)} %bitcast.21), calls=%async_computation.2 | async-start | bytes 262144 | tf_op jit(solution)/shard_map/all_to_all | solution.py:149
  112.7 26.8 %copy-start.9 = (f32[1,24]{1,0:T(1,128)S(1)}, f32[1,24]{1,0:T(1,128)}, u32[]{:S(2)}) copy-start(f32[1,24]{1,0:T(1,128)} %get-tuple-element.69) | copy-start | bytes 292
  130.5 26.1 %all-to-all-start = ((f32[32,16,128]{2,1,0:T(8,128)}), f32[32,16,128]{2,1,0:T(8,128)S(1)}, u32[]{:S(2)}, u32[]{:S(2)}) async-start(f32[32,16,128]{2,1,0:T(8,128)} %bitcast.13), calls=%async_computation | async-start | bytes 524288 | tf_op jit(solution)/shard_map/all_to_all | solution.py:146
  164.9 25.1 %all-to-all-start.1 = ((f32[16,32,128]{2,0,1:T(8,128)}), f32[16,32,128]{2,0,1:T(8,128)S(1)}, u32[]{:S(2)}, u32[]{:S(2)}) async-start(f32[16,32,128]{2,0,1:T(8,128)} %copy.17), calls=%async_computation.1 | async-start | bytes 524288 | tf_op jit(solution)/shard_map/all_to_all | solution.py:165
  (11 other events, 230.0 us)
where the time goes:
time: 192 us; the launch traced here: 191 us
  starting transfers between devices  88.8 us (46%)
  waiting for transfers between devices  63.4 us (33%)
  local copies, waits for them, and re-layouts  14 us (7%)
  other arithmetic  12.6 us (7%)
  matrix products  10.4 us (5%)
    ppermute x8, starting transfers between devices, shifted(): lax.ppermute(shard, axis, [(i, (i + by) % count) for i in range(count)])  32.3 us
    all_to_all x1, starting transfers between devices, body(): lax.all_to_all(speed_column, 'coef', split_axis=0, concat_axis=1, tiled=T...  17.9 us
    ppermute x4, starting transfers between devices, extended(): lax.ppermute(lax.slice_in_dim(block, block.shape[dim] - width, None, axis...  17.5 us
    all_to_all x1, waiting for transfers between devices, body(): lax.all_to_all(source_state, 'coef', split_axis=0, concat_axis=1, tiled=T...  15.6 us
    all_to_all x1, waiting for transfers between devices, body(): lax.all_to_all(adj_cells, 'coef', split_axis=1, concat_axis=0, tiled=True)  14.8 us
    all_to_all x1, waiting for transfers between devices, body(): lax.all_to_all(speed_column, 'coef', split_axis=0, concat_axis=1, tiled=T...  14.7 us
    all_to_all x1, waiting for transfers between devices, body(): lax.all_to_all(mu_field, 'coef', split_axis=0, concat_axis=1, tiled=True)  13.5 us
    ppermute x4, starting transfers between devices, extended(): lax.ppermute(lax.slice_in_dim(block, 0, width, axis=dim), axis, backward)  9.26 us
  transfers between devices with their start and end apart: 20, of which 8 were waited for; matrix products, arithmetic and copies ran while one was open for 13% of the time, Pallas kernels for 0%

commit v1 on v0

v1 whole, which is shorter than its diff:
```python
import functools
import math

import jax
import jax.numpy as jnp
import ml_dtypes
import numpy as np
from jax import lax
from jax.experimental import pallas as pl
from jax.experimental.pallas import tpu as pltpu
from jax.sharding import PartitionSpec as P

CYZ = 128
NH = 16
QP = 24
K = 4096
PLANES = 4
SLABS = 16
OWNERS = 32
CELLS = 16
WIDTH = 128
POINTS = QP * QP

section_weights = (0.25, 1.0 / 3.0, 0.5, 1.0)
quad_half = 4.5
fene_limit = 64.0
time_step = 0.005
weight_cube = (2.0 * quad_half / QP) ** 3
code_top = 32600.0
f32 = jnp.float32
bf16 = jnp.bfloat16
MESH = pl.DeviceIdType.MESH


def split_table(table):
    high = table.astype(np.float32).astype(ml_dtypes.bfloat16)
    low = (table - high.astype(np.float64)).astype(np.float32).astype(ml_dtypes.bfloat16)
    return np.stack([high, low])


@functools.cache
def tables():
    x = quad_half * (2.0 * np.arange(QP) + 1.0 - QP) / QP
    rows = [np.exp(-0.5 * x * x) * math.pi ** (-0.25)]
    rows.append(math.sqrt(2.0) * x * rows[0])
    for m in range(1, NH - 1):
        rows.append(
            math.sqrt(2.0 / (m + 1.0)) * x * rows[m] - math.sqrt(m / (m + 1.0)) * rows[m - 1]
        )
    h = np.stack(rows)
    inner = np.kron(h, h)
    outer = np.kron(h.T, np.eye(CELLS))
    xb = np.repeat(x, QP)
    xd = np.tile(x, QP)
    square = x[:, None] ** 2 + (xb**2 + xd**2)[None, :]
    ratio = time_step / (1.0 - square / fene_limit)
    zero = np.zeros(POINTS)
    one = np.ones(POINTS)
    moments = np.zeros((3, 16, POINTS))
    moments[0, [4, 5, 7, 8]] = [xb * xb, xb * xd, xb * xd, xd * xd]
    moments[1, [1, 2, 3, 6]] = [xb, xd, xb, xd]
    moments[2, 0] = one
    points = np.stack([xb, xd, xb * xb, xb * xd, xd * xd, zero, zero, zero])
    return (
        x,
        split_table(outer),
        split_table(inner),
        split_table(np.ascontiguousarray(inner.T)),
        split_table(np.ascontiguousarray(outer.T)),
        ratio.astype(np.float32),
        points.astype(np.float32),
        moments.astype(np.float32),
    )


def halves(value):
    high = value.astype(bf16)
    return high, (value - high.astype(f32)).astype(bf16)


def product(left, right):
    total = None
    for i, a in enumerate(left):
        for j, b in enumerate(right):
            if i + j < 2:
                part = jnp.dot(a, b, preferred_element_type=f32)
                total = part if total is None else total + part
    return total


def encode(low, high):
    top = jnp.max(jnp.maximum(jnp.abs(low), jnp.abs(high)), axis=0, keepdims=True)
    level = jnp.ceil(jnp.log2(jnp.maximum(top, 1e-30)) * 8.0)
    unit = jnp.exp2(level * -0.125) * code_top
    low_code = jnp.round(low * unit).astype(jnp.int32)
    high_code = jnp.round(high * unit).astype(jnp.int32)
    word = jnp.bitwise_or(lax.shift_left(high_code, 16), jnp.bitwise_and(low_code, 0xFFFF))
    return word, level.astype(jnp.int32)


def decode(word, level, factor):
    unit = jnp.exp2(level.astype(f32) * 0.125) * (factor / code_top)
    low = lax.shift_right_arithmetic(lax.shift_left(word, 16), 16).astype(f32) * unit
    high = lax.shift_right_arithmetic(word, 16).astype(f32) * unit
    return low, high


def kernel(
    nodes,
    cot, tst, src, cou, cod, strain,
    outer_hbm, inner_hbm, inner_t_hbm, outer_t_hbm, ratio_ref, points_ref, moments_ref,
    out_source, out_strain, out_courant,
    gbuf, tbuf, scbuf, sct_buf, acc_buf,
    src_recv, mu_send, mu_recv, back_send, back_recv, speed_send, speed_recv,
    outer_ref, inner_ref, inner_t_ref, outer_t_ref,
    u_buf, es_buf, square_buf, line_buf, column_buf,
    local_sem, halo_send, halo_recv, all_send, all_recv,
):
    me = lax.axis_index("coef")
    slab = lax.axis_index("slab")
    above = lax.rem(slab + 1, SLABS)
    below = lax.rem(slab + SLABS - 1, SLABS)
    rows = PLANES * CYZ

    loads = [
        pltpu.make_async_copy(cot, gbuf.at[pl.ds(rows, rows)], local_sem.at[0]),
        pltpu.make_async_copy(tst, tbuf.at[pl.ds(rows, rows)], local_sem.at[1]),
        pltpu.make_async_copy(outer_hbm, outer_ref, local_sem.at[2]),
        pltpu.make_async_copy(inner_hbm, inner_ref, local_sem.at[3]),
        pltpu.make_async_copy(inner_t_hbm, inner_t_ref, local_sem.at[4]),
        pltpu.make_async_copy(outer_t_hbm, outer_t_ref, local_sem.at[5]),
        pltpu.make_async_copy(
            src.at[pl.ds(pl.multiple_of(me * CELLS, CELLS), CELLS)],
            src_recv.at[lax.rem(me, 2), lax.div(me, 2)],
            local_sem.at[6],
        ),
    ]
    barrier = pltpu.get_barrier_semaphore()

    def greet(off, _):
        pl.semaphore_signal(
            barrier, inc=1, device_id={"coef": lax.rem(me + off, OWNERS)}, device_id_type=MESH
        )
        return 0

    pl.semaphore_signal(barrier, inc=1, device_id={"slab": above}, device_id_type=MESH)
    pl.semaphore_signal(barrier, inc=1, device_id={"slab": below}, device_id_type=MESH)
    lax.fori_loop(1, OWNERS, greet, 0)
    for load in loads:
        load.start()
    scbuf[1] = jnp.where(cod[...] == 1, -cou[...], cou[...])
    pl.semaphore_wait(barrier, OWNERS + 1)

    halos = []
    for way, target, place in ((0, above, 0), (1, below, 2)):
        here = pl.ds(place * rows, rows)
        for kind, source, dest in (
            (0, scbuf.at[1], scbuf.at[place]),
            (1, tst, tbuf.at[here]),
            (2, cot, gbuf.at[here]),
        ):
            halos.append(
                pltpu.make_async_remote_copy(
                    src_ref=source,
                    dst_ref=dest,
                    send_sem=halo_send.at[way, kind],
                    recv_sem=halo_recv.at[way, kind],
                    device_id={"slab": target},
                    device_id_type=MESH,
                )
            )
    for halo in halos:
        halo.start()

    my_half, my_mode = lax.rem(me, 2), lax.div(me, 2)

    def send_source(off, _):
        dest = lax.rem(me + off, OWNERS)
        pltpu.make_async_remote_copy(
            src_ref=src.at[pl.ds(pl.multiple_of(dest * CELLS, CELLS), CELLS)],
            dst_ref=src_recv.at[my_half, my_mode],
            send_sem=all_send.at[0],
            recv_sem=all_recv.at[0],
            device_id={"coef": dest},
            device_id_type=MESH,
        ).start()
        return 0

    lax.fori_loop(1, OWNERS, send_source, 0)

    column_buf[...] = jnp.zeros((128, 128), f32)
    column_buf[0:9, 0:16] = strain[...]
    turned = jnp.transpose(column_buf[...])[0:16]
    col = [turned[:, p : p + 1] for p in range(9)]
    pts = [points_ref[n : n + 1] for n in range(5)]
    line_buf[...] = (col[1] + col[3]) * pts[0] + (col[2] + col[6]) * pts[1]
    square_buf[...] = col[4] * pts[2] + (col[5] + col[7]) * pts[3] + col[8] * pts[4]

    loads[0].wait()
    loads[1].wait()
    for halo in halos:
        halo.wait()
    signed = jnp.concatenate([scbuf[0], scbuf[1], scbuf[2], jnp.zeros((116, 128), f32)], axis=0)
    sct_buf[...] = jnp.transpose(signed)

    def chunk(step, _):
        part = lax.rem(me + step, 8)
        mu_parts = []
        for h in range(2):
            y = pl.multiple_of(part * 16 + h * 8, 8)
            sct = sct_buf[pl.ds(y, 8), :]
            wide = [jnp.broadcast_to(sct[:, p : p + 1], (8, WIDTH)) for p in range(12)]
            upper = [c < 0.0 for c in wide]
            c0 = [jnp.maximum(c, 0.0) for c in wide]
            c1 = [jnp.maximum(-c, 0.0) for c in wide]
            speed = [jnp.abs(c) for c in wide]
            s0 = [
                tbuf[pl.ds(pl.multiple_of(p * CYZ + part * 16, 16), 16), :].astype(f32)[
                    h * 8 : h * 8 + 8
                ]
                for p in range(12)
            ]
            s = dict(enumerate(s0))
            own = []
            for n in range(4):
                edge = {p: s[p + 1] - s[p] for p in range(n, 11 - n)}
                change = {p: jnp.where(upper[p], edge[p], edge[p - 1]) for p in range(n + 1, 11 - n)}
                own.append([change[p] for p in range(4, 8)])
                if n < 3:
                    s = {p: s0[p] - section_weights[n] * speed[p] * change[p] for p in change}
            g = {p: gbuf[pl.ds(p * CYZ + y, 8), :] for p in range(12)}
            mu = [g[p] for p in range(4, 8)]
            acc = [None] * 4
            for k, n in enumerate((3, 2, 1, 0)):
                for p in range(4):
                    term = section_weights[n] * (g[p + 4] * own[n][p])
                    acc[p] = term if acc[p] is None else acc[p] + term
                flow = {p: c1[p] * g[p] + c0[p + 1] * g[p + 1] for p in range(k, 11 - k)}
                g = {p: section_weights[n] * (flow[p] - flow[p - 1]) for p in range(k + 1, 11 - k)}
                mu = [mu[p] + g[p + 4] for p in range(4)]
            for p in range(4):
                acc_buf[p, pl.ds(y, 8), :] = acc[p]
            mu_parts.append(mu)
        for p in range(4):
            dest = p * 8 + part
            word, level = encode(mu_parts[0][p], mu_parts[1][p])
            mu_send[dest, 0:8, :] = word
            mu_send[dest, 8:9, :] = level
            where_to = mu_recv.at[my_half, my_mode]

            @pl.when(dest != me)
            def _():
                pltpu.make_async_remote_copy(
                    src_ref=mu_send.at[dest],
                    dst_ref=where_to,
                    send_sem=all_send.at[1],
                    recv_sem=all_recv.at[1],
                    device_id={"coef": dest},
                    device_id_type=MESH,
                ).start()

            @pl.when(dest == me)
            def _():
                pltpu.make_async_copy(mu_send.at[dest], where_to, local_sem.at[7]).start()

        return 0

    lax.fori_loop(0, 8, chunk, 0)

    ones = jnp.ones((8, WIDTH), bf16)
    for p in range(4):
        total = None
        for piece in halves(acc_buf[p]):
            part = lax.dot_general(
                ones, piece, (((1,), (1,)), ((), ())), preferred_element_type=f32
            )
            total = part if total is None else total + part
        speed_send[p] = total

    def send_speed(off, _):
        dest = lax.rem(me + off, OWNERS)
        pltpu.make_async_remote_copy(
            src_ref=speed_send.at[lax.div(dest, 8), pl.ds(0, 1)],
            dst_ref=speed_recv.at[me, pl.ds(0, 1)],
            send_sem=all_send.at[2],
            recv_sem=all_recv.at[2],
            device_id={"coef": dest},
            device_id_type=MESH,
        ).start()
        return 0

    lax.fori_loop(1, OWNERS, send_speed, 0)
    speed_recv[me, 0:1, :] = speed_send[lax.div(me, 8), 0:1, :]

    def wait_all(ref, sem):
        pltpu.make_async_copy(ref, ref, sem).wait()

    src_31 = src.at[pl.ds(0, (OWNERS - 1) * CELLS)]
    wait_all(src_31, all_recv.at[0])
    for n in (2, 3, 4, 5, 6):
        loads[n].wait()
    outer = (outer_ref[0], outer_ref[1])
    inner = (inner_ref[0], inner_ref[1])
    source = jnp.concatenate(
        [src_recv[0].reshape(256, WIDTH), src_recv[1].reshape(256, WIDTH)], axis=1
    )
    es_buf[...] = product(halves(product(outer, (source,))), inner)

    wait_all(mu_send.at[pl.ds(0, OWNERS - 1)], all_recv.at[1])
    pltpu.make_async_copy(mu_send.at[0], mu_send.at[0], local_sem.at[7]).wait()
    mu_high, mu_low = [], []
    for half in range(2):
        high_rows, low_rows = [], []
        for mode in range(NH):
            block = jnp.concatenate(
                decode(
                    mu_recv[half, mode, 0:8, :], mu_recv[half, mode, 8:9, :], weight_cube
                ),
                axis=0,
            )
            high, low = halves(block)
            high_rows.append(high)
            low_rows.append(low)
        mu_high.append(jnp.concatenate(high_rows, axis=0))
        mu_low.append(jnp.concatenate(low_rows, axis=0))
    mu_cells = (jnp.concatenate(mu_high, axis=1), jnp.concatenate(mu_low, axis=1))
    first = halves(product(outer, mu_cells))
    inner_t = (inner_t_ref[0], inner_t_ref[1])
    outer_t = (outer_t_ref[0], outer_t_ref[1])
    line, square = line_buf[...], square_buf[...]
    back = []
    for block in range(3):
        here = slice(block * 128, block * 128 + 128)
        values = product((first[0][here], first[1][here]), inner)
        u_buf[here, :] = values
        weighted = []
        for n in range(8):
            a = block * 8 + n
            u = values[n * CELLS : n * CELLS + CELLS]
            x = float(nodes[a])
            form = (square + x * (line + x * col[0])) * ratio_ref[a : a + 1, :]
            weighted.append(u + u * form)
        back.append(product(halves(jnp.concatenate(weighted, axis=0)), inner_t))
    adj = product(outer_t, halves(jnp.concatenate(back, axis=0)))
    for mode in range(NH):
        for half in range(2):
            dest = 2 * mode + half
            block = adj[mode * CELLS : mode * CELLS + CELLS, half * WIDTH : half * WIDTH + WIDTH]
            word, level = encode(block[0:8], block[8:16])
            back_send[dest, 0:8, :] = word
            back_send[dest, 8:9, :] = level

    def send_back(off, _):
        dest = lax.rem(me + off, OWNERS)
        pltpu.make_async_remote_copy(
            src_ref=back_send.at[dest],
            dst_ref=back_recv.at[me],
            send_sem=all_send.at[3],
            recv_sem=all_recv.at[3],
            device_id={"coef": dest},
            device_id_type=MESH,
        ).start()
        return 0

    lax.fori_loop(1, OWNERS, send_back, 0)
    own_back = pltpu.make_async_copy(back_send.at[me], back_recv.at[me], local_sem.at[8])
    own_back.start()

    sums = [None, None, None]
    for a in range(QP):
        here = slice(a * CELLS, a * CELLS + CELLS)
        y = u_buf[here, :] * es_buf[here, :] * ratio_ref[a : a + 1, :]
        x = float(nodes[a])
        for n, term in enumerate((y, x * y, (x * x) * y)):
            sums[n] = term if sums[n] is None else sums[n] + term
    strain_sum = None
    for n in range(3):
        part = lax.dot_general(
            moments_ref[n],
            sums[n],
            (((1,), (1,)), ((), ())),
            precision=lax.Precision.HIGHEST,
            preferred_element_type=f32,
        )
        strain_sum = part if strain_sum is None else strain_sum + part
    out_strain[...] = strain_sum[0:9, :]

    wait_all(speed_recv.at[pl.ds(0, OWNERS - 1), pl.ds(0, 1)], all_recv.at[2])
    total = speed_recv[0, 0:1, :]
    for n in range(1, OWNERS):
        total = total + speed_recv[n, 0:1, :]
    start = lax.rem(me, 8) * CELLS
    total = pltpu.roll(jnp.broadcast_to(total, (8, 128)), lax.rem(128 - start, 128), 1)
    out_courant[...] = total[0:1, 0:CELLS] * (-1.0 / math.sqrt(K))

    own_back.wait()
    wait_all(back_send.at[pl.ds(0, OWNERS - 1)], all_recv.at[3])
    for n in range(OWNERS):
        low, high = decode(back_recv[n, 0:8, :], back_recv[n, 8:9, :], 1.0)
        out_source[n * CELLS : n * CELLS + 8, :] = low
        out_source[n * CELLS + 8 : n * CELLS + 16, :] = high

    wait_all(src_31, all_send.at[0])
    wait_all(mu_send.at[pl.ds(0, OWNERS - 1)], all_send.at[1])
    wait_all(speed_recv.at[pl.ds(0, OWNERS - 1), pl.ds(0, 1)], all_send.at[2])
    wait_all(back_send.at[pl.ds(0, OWNERS - 1)], all_send.at[3])


def body(cotangent, transport_state, source_state, courant, upwind_codes, strain_rate):
    nodes, *constants = tables()
    rows = PLANES * CYZ
    anywhere = pl.BlockSpec(memory_space=pl.ANY)
    vmem = pl.BlockSpec(memory_space=pltpu.VMEM)
    adj_source, adj_strain, adj_courant = pl.pallas_call(
        functools.partial(kernel, nodes),
        out_shape=(
            jax.ShapeDtypeStruct((rows, WIDTH), f32),
            jax.ShapeDtypeStruct((9, CELLS), f32),
            jax.ShapeDtypeStruct((1, CELLS), f32),
        ),
        in_specs=[anywhere] * 3 + [vmem] * 3 + [anywhere] * 4 + [vmem] * 3,
        out_specs=(vmem, vmem, vmem),
        scratch_shapes=[
            pltpu.VMEM((3 * rows, WIDTH), f32),
            pltpu.VMEM((3 * rows, WIDTH), bf16),
            pltpu.VMEM((3, PLANES, CYZ), f32),
            pltpu.VMEM((128, 128), f32),
            pltpu.VMEM((PLANES, CYZ, WIDTH), f32),
            pltpu.VMEM((2, NH, CELLS, WIDTH), bf16),
            pltpu.VMEM((OWNERS, 9, WIDTH), jnp.int32),
            pltpu.VMEM((2, NH, 9, WIDTH), jnp.int32),
            pltpu.VMEM((OWNERS, 9, WIDTH), jnp.int32),
            pltpu.VMEM((OWNERS, 9, WIDTH), jnp.int32),
            pltpu.VMEM((PLANES, 8, WIDTH), f32),
            pltpu.VMEM((OWNERS, 8, WIDTH), f32),
            pltpu.VMEM((2, QP * CELLS, NH * CELLS), bf16),
            pltpu.VMEM((2, NH * NH, POINTS), bf16),
            pltpu.VMEM((2, POINTS, NH * NH), bf16),
            pltpu.VMEM((2, NH * CELLS, QP * CELLS), bf16),
            pltpu.VMEM((QP * CELLS, POINTS), f32),
            pltpu.VMEM((QP * CELLS, POINTS), f32),
            pltpu.VMEM((CELLS, POINTS), f32),
            pltpu.VMEM((CELLS, POINTS), f32),
            pltpu.VMEM((128, 128), f32),
            pltpu.SemaphoreType.DMA((9,)),
            pltpu.SemaphoreType.DMA((2, 3)),
            pltpu.SemaphoreType.DMA((2, 3)),
            pltpu.SemaphoreType.DMA((4,)),
            pltpu.SemaphoreType.DMA((4,)),
        ],
        compiler_params=pltpu.CompilerParams(
            collective_id=0, has_side_effects=True, vmem_limit_bytes=40 * 2**20
        ),
    )(
        cotangent,
        transport_state,
        source_state,
        courant.reshape(PLANES, CYZ),
        upwind_codes.reshape(PLANES, CYZ),
        strain_rate,
        *[jnp.asarray(table) for table in constants],
    )
    return adj_source, adj_strain, adj_courant.reshape(CELLS)


def solution(mesh):
    placed = (
        P("slab", "coef"),
        P("slab", "coef"),
        P("slab", "coef"),
        P("slab"),
        P("slab"),
        P(None, ("slab", "coef")),
    )
    return jax.shard_map(
        body,
        mesh=mesh,
        in_specs=placed,
        out_specs=(P("slab", "coef"), P(None, ("slab", "coef")), P(("slab", "coef"))),
        check_vma=False,
    )
```

time: 192 us -> 64.3 us (0.33)
  the two profiles are of different devices: /device:TPU:24 before, /device:TPU:2 now
where the time goes in v1:
time: 64.3 us; the launch traced here: 63.7 us
  Pallas kernels  49.8 us (77%)
  local copies, waits for them, and re-layouts  13.2 us (21%)
  between operations  0.66 us (1%)
    pallas_call x1, Pallas kernels, body(): pl.pallas_call(functools.partial(kernel, nodes), out_shape=(jax.ShapeDtyp...  49.8 us
    unnamed x29, local copies, waits for them, and re-layouts  13.2 us

profile of v1, /device:TPU:2, one launch (start us, length us, event | category | flops | bytes accessed | tf_op | source)
XLA Modules:
  0.0 63.7 jit_solution(16110241037496638398)
XLA Ops:
  0.6 0.0 copy-start.11
  0.6 0.7 %copy-done.11 = f32[512]{0:T(512)S(1)} copy-done((f32[512]{0:T(512)S(1)}, f32[512]{0:T(512)}, u32[]{:S(2)}) %copy-start.11) | copy-done | bytes 2072
  1.3 0.0 copy-start
  1.3 1.1 %copy-done = bf16[2,256,576]{2,1,0:T(8,128)(2,1)S(1)} copy-done((bf16[2,256,576]{2,1,0:T(8,128)(2,1)S(1)}, bf16[2,256,576]{2,1,0:T(8,128)(2,1)}, u32[]{:S(2)}) %copy-start) | copy-done | bytes 589848
  2.4 0.0 copy-start.1
  2.4 1.1 %copy-done.1 = bf16[2,576,256]{2,1,0:T(8,128)(2,1)S(1)} copy-done((bf16[2,576,256]{2,1,0:T(8,128)(2,1)S(1)}, bf16[2,576,256]{2,1,0:T(8,128)(2,1)}, u32[]{:S(2)}) %copy-start.1) | copy-done | bytes 589848
  3.5 0.0 copy-start.2
  3.5 1.0 %copy-done.2 = bf16[2,256,384]{2,1,0:T(8,128)(2,1)S(1)} copy-done((bf16[2,256,384]{2,1,0:T(8,128)(2,1)S(1)}, bf16[2,256,384]{2,1,0:T(8,128)(2,1)}, u32[]{:S(2)}) %copy-start.2) | copy-done | bytes 393240
  4.5 0.0 copy-start.3
  4.5 1.0 %copy-done.3 = bf16[2,384,256]{2,1,0:T(8,128)(2,1)S(1)} copy-done((bf16[2,384,256]{2,1,0:T(8,128)(2,1)S(1)}, bf16[2,384,256]{2,1,0:T(8,128)(2,1)}, u32[]{:S(2)}) %copy-start.3) | copy-done | bytes 393240
  5.5 0.0 copy-start.4
  5.5 0.9 %copy-done.4 = f32[512,128]{1,0:T(8,128)S(1)} copy-done((f32[512,128]{1,0:T(8,128)S(1)}, f32[512,128]{1,0:T(8,128)}, u32[]{:S(2)}) %copy-start.4) | copy-done | bytes 262168
  6.4 0.0 copy-start.5
  6.4 0.9 %copy-done.5 = bf16[512,128]{1,0:T(8,128)(2,1)S(1)} copy-done((bf16[512,128]{1,0:T(8,128)(2,1)S(1)}, bf16[512,128]{1,0:T(8,128)(2,1)}, u32[]{:S(2)}) %copy-start.5) | copy-done | bytes 131096
  7.3 0.9 %copy-done.6 = bf16[512,128]{1,0:T(8,128)(2,1)S(1)} copy-done((bf16[512,128]{1,0:T(8,128)(2,1)S(1)}, bf16[512,128]{1,0:T(8,128)(2,1)}, u32[]{:S(2)}) %copy-start.6) | copy-done | bytes 131096
  8.2 0.9 %copy-done.7 = f32[3,16,576]{2,1,0:T(8,128)S(1)} copy-done((f32[3,16,576]{2,1,0:T(8,128)S(1)}, f32[3,16,576]{2,1,0:T(8,128)}, u32[]{:S(2)}) %copy-start.7) | copy-done | bytes 110616
  9.1 0.8 %copy-done.8 = f32[24,576]{1,0:T(8,128)S(1)} copy-done((f32[24,576]{1,0:T(8,128)S(1)}, f32[24,576]{1,0:T(8,128)}, u32[]{:S(2)}) %copy-start.8) | copy-done | bytes 55320
  10.0 0.7 %copy-done.9 = f32[8,576]{1,0:T(8,128)S(1)} copy-done((f32[8,576]{1,0:T(8,128)S(1)}, f32[8,576]{1,0:T(8,128)}, u32[]{:S(2)}) %copy-start.9) | copy-done | bytes 18456
  10.7 0.7 %copy-done.10 = f32[9,16]{1,0:T(8,128)S(1)} copy-done((f32[9,16]{1,0:T(8,128)S(1)}, f32[9,16]{1,0:T(8,128)}, u32[]{:S(2)}) %copy-start.10) | copy-done | bytes 600
  11.4 0.7 %copy-done.12 = s32[512]{0:T(512)S(1)} copy-done((s32[512]{0:T(512)S(1)}, s32[512]{0:T(512)}, u32[]{:S(2)}) %copy-start.12) | copy-done | bytes 2072
  12.1 49.8 %shard_map.148 = (f32[512,128]{1,0:T(8,128)S(1)}, f32[9,16]{1,0:T(8,128)S(1)}, f32[1,16]{1,0:T(1,128)S(1)}) custom-call(f32[512,128]{1,0:T(8,128)S(1)} %copy-done.4, bf16[512,128]{1,0:T(8,128)(2,1)S(1)} %copy-done.5, bf16[512,128]{1,0:T(8,128)(2,1)S(1)} %copy-done.6, f32[4,128]{1,0:T(4,128)S(1)} %bitcast.3, s32[4,128]{1,0:T(4,128)S(1)} %bitcast.4, ...), custom_call_target="tpu_custom_call" | custom-call | tf_op jit(solution)/shard_map/pallas_call | solution.py:414
  61.9 0.7 %copy.19 = f32[512,128]{1,0:T(8,128)} copy(f32[512,128]{1,0:T(8,128)S(1)} %get-tuple-element.12) | data formatting | bytes 524288
  62.6 0.6 copy.20
  63.2 0.5 copy.21
  (6 shorter events, 0.0 us)
Async XLA Ops:
  0.6 0.7 %copy-start.11 = (f32[512]{0:T(512)S(1)}, f32[512]{0:T(512)}, u32[]{:S(2)}) copy-start(f32[512]{0:T(512)} %param.16) | copy-start | bytes 6148
  1.3 1.1 %copy-start = (bf16[2,256,576]{2,1,0:T(8,128)(2,1)S(1)}, bf16[2,256,576]{2,1,0:T(8,128)(2,1)}, u32[]{:S(2)}) copy-start(bf16[2,256,576]{2,1,0:T(8,128)(2,1)} %constant.15.clone.inner_hbm) | copy-start | bytes 1769476
  2.4 1.1 %copy-start.1 = (bf16[2,576,256]{2,1,0:T(8,128)(2,1)S(1)}, bf16[2,576,256]{2,1,0:T(8,128)(2,1)}, u32[]{:S(2)}) copy-start(bf16[2,576,256]{2,1,0:T(8,128)(2,1)} %constant.16.clone.inner_t_hbm) | copy-start | bytes 1769476
  3.5 1.0 %copy-start.2 = (bf16[2,256,384]{2,1,0:T(8,128)(2,1)S(1)}, bf16[2,256,384]{2,1,0:T(8,128)(2,1)}, u32[]{:S(2)}) copy-start(bf16[2,256,384]{2,1,0:T(8,128)(2,1)} %constant.17.clone.outer_t_hbm) | copy-start | bytes 1179652
  4.5 1.0 %copy-start.3 = (bf16[2,384,256]{2,1,0:T(8,128)(2,1)S(1)}, bf16[2,384,256]{2,1,0:T(8,128)(2,1)}, u32[]{:S(2)}) copy-start(bf16[2,384,256]{2,1,0:T(8,128)(2,1)} %constant.14.clone.outer_hbm) | copy-start | bytes 1179652
  5.5 0.9 %copy-start.4 = (f32[512,128]{1,0:T(8,128)S(1)}, f32[512,128]{1,0:T(8,128)}, u32[]{:S(2)}) copy-start(f32[512,128]{1,0:T(8,128)} %cot.1) | copy-start | bytes 786436
  6.4 0.9 %copy-start.5 = (bf16[512,128]{1,0:T(8,128)(2,1)S(1)}, bf16[512,128]{1,0:T(8,128)(2,1)}, u32[]{:S(2)}) copy-start(bf16[512,128]{1,0:T(8,128)(2,1)} %tst.1) | copy-start | bytes 393220
  7.3 0.9 %copy-start.6 = (bf16[512,128]{1,0:T(8,128)(2,1)S(1)}, bf16[512,128]{1,0:T(8,128)(2,1)}, u32[]{:S(2)}) copy-start(bf16[512,128]{1,0:T(8,128)(2,1)} %src.1) | copy-start | bytes 393220
  8.2 0.9 %copy-start.7 = (f32[3,16,576]{2,1,0:T(8,128)S(1)}, f32[3,16,576]{2,1,0:T(8,128)}, u32[]{:S(2)}) copy-start(f32[3,16,576]{2,1,0:T(8,128)} %constant.20.clone.moments_ref) | copy-start | bytes 331780
  9.1 0.8 %copy-start.8 = (f32[24,576]{1,0:T(8,128)S(1)}, f32[24,576]{1,0:T(8,128)}, u32[]{:S(2)}) copy-start(f32[24,576]{1,0:T(8,128)} %constant.18.clone.ratio_ref) | copy-start | bytes 165892
  10.0 0.7 %copy-start.9 = (f32[8,576]{1,0:T(8,128)S(1)}, f32[8,576]{1,0:T(8,128)}, u32[]{:S(2)}) copy-start(f32[8,576]{1,0:T(8,128)} %constant.19.clone.points_ref) | copy-start | bytes 55300
  10.7 0.7 %copy-start.10 = (f32[9,16]{1,0:T(8,128)S(1)}, f32[9,16]{1,0:T(8,128)}, u32[]{:S(2)}) copy-start(f32[9,16]{1,0:T(8,128)} %strain.1) | copy-start | bytes 1732
  11.4 0.7 %copy-start.12 = (s32[512]{0:T(512)S(1)}, s32[512]{0:T(512)}, u32[]{:S(2)}) copy-start(s32[512]{0:T(512)} %param.17) | copy-start | bytes 6148

commit v2 on v1

v2 whole, which is shorter than its diff:
```python
import functools
import math

import jax
import jax.numpy as jnp
import ml_dtypes
import numpy as np
from jax import lax
from jax.experimental import pallas as pl
from jax.experimental.pallas import tpu as pltpu
from jax.sharding import PartitionSpec as P

CYZ = 128
NH = 16
QP = 24
K = 4096
PLANES = 4
SLABS = 16
OWNERS = 32
CELLS = 16
WIDTH = 128
POINTS = QP * QP

section_weights = (0.25, 1.0 / 3.0, 0.5, 1.0)
quad_half = 4.5
fene_limit = 64.0
time_step = 0.005
weight_cube = (2.0 * quad_half / QP) ** 3
code_top = 32600.0
f32 = jnp.float32
bf16 = jnp.bfloat16
MESH = pl.DeviceIdType.MESH


def split_table(table):
    high = table.astype(np.float32).astype(ml_dtypes.bfloat16)
    low = (table - high.astype(np.float64)).astype(np.float32).astype(ml_dtypes.bfloat16)
    return np.stack([high, low])


@functools.cache
def tables():
    x = quad_half * (2.0 * np.arange(QP) + 1.0 - QP) / QP
    rows = [np.exp(-0.5 * x * x) * math.pi ** (-0.25)]
    rows.append(math.sqrt(2.0) * x * rows[0])
    for m in range(1, NH - 1):
        rows.append(
            math.sqrt(2.0 / (m + 1.0)) * x * rows[m] - math.sqrt(m / (m + 1.0)) * rows[m - 1]
        )
    h = np.stack(rows)
    inner = np.kron(h, h)
    outer = np.kron(h.T, np.eye(CELLS))
    xb = np.repeat(x, QP)
    xd = np.tile(x, QP)
    square = x[:, None] ** 2 + (xb**2 + xd**2)[None, :]
    ratio = time_step / (1.0 - square / fene_limit)
    zero = np.zeros(POINTS)
    one = np.ones(POINTS)
    moments = np.zeros((3, 16, POINTS))
    moments[0, [4, 5, 7, 8]] = [xb * xb, xb * xd, xb * xd, xd * xd]
    moments[1, [1, 2, 3, 6]] = [xb, xd, xb, xd]
    moments[2, 0] = one
    points = np.stack([xb, xd, xb * xb, xb * xd, xd * xd, zero, zero, zero])
    return (
        x,
        split_table(outer),
        split_table(inner),
        split_table(np.ascontiguousarray(inner.T)),
        split_table(np.ascontiguousarray(outer.T)),
        ratio.astype(np.float32),
        points.astype(np.float32),
        moments.astype(np.float32),
    )


def halves(value):
    high = value.astype(bf16)
    return high, (value - high.astype(f32)).astype(bf16)


def product(left, right):
    total = None
    for i, a in enumerate(left):
        for j, b in enumerate(right):
            if i + j < 2:
                part = jnp.dot(a, b, preferred_element_type=f32)
                total = part if total is None else total + part
    return total


def encode(low, high):
    top = jnp.max(jnp.maximum(jnp.abs(low), jnp.abs(high)), axis=0, keepdims=True)
    level = jnp.ceil(jnp.log2(jnp.maximum(top, 1e-30)) * 8.0)
    unit = jnp.exp2(level * -0.125) * code_top
    low_code = jnp.round(low * unit).astype(jnp.int32)
    high_code = jnp.round(high * unit).astype(jnp.int32)
    word = jnp.bitwise_or(lax.shift_left(high_code, 16), jnp.bitwise_and(low_code, 0xFFFF))
    return word, level.astype(jnp.int32)


def decode(word, level, factor):
    unit = jnp.exp2(level.astype(f32) * 0.125) * (factor / code_top)
    low = lax.shift_right_arithmetic(lax.shift_left(word, 16), 16).astype(f32) * unit
    high = lax.shift_right_arithmetic(word, 16).astype(f32) * unit
    return low, high


def sum_code(value):
    size = jnp.abs(value)
    code = jnp.round((jnp.log2(jnp.maximum(size, 1e-30)) + 100.0) * 2.0**20).astype(jnp.int32)
    code = jnp.where(size < 1e-30, 0, code)
    return jnp.where(value < 0.0, -code, code)


def sum_value(code):
    size = jnp.exp2(jnp.abs(code).astype(f32) * 2.0**-20 - 100.0)
    size = jnp.where(code == 0, 0.0, size)
    return jnp.where(code < 0, -size, size)


def kernel(
    nodes,
    cot, tst, src, cou_hbm, cod_hbm, strain_hbm,
    outer_hbm, inner_hbm, inner_t_hbm, outer_t_hbm, ratio_hbm, points_hbm, moments_hbm,
    back_recv, out_strain, out_courant,
    gbuf, tbuf, scbuf, sct_buf,
    src_recv, mu_send, mu_recv, back_send,
    cou, cod, strain,
    outer_ref, inner_ref, inner_t_ref, outer_t_ref, ratio_ref, points_ref, moments_ref,
    u_buf, es_buf, square_buf, line_buf, column_buf, strain_buf, courant_buf, courant_out,
    local_sem, halo_send, halo_recv, all_send, all_recv,
):
    me = lax.axis_index("coef")
    slab = lax.axis_index("slab")
    above = lax.rem(slab + 1, SLABS)
    below = lax.rem(slab + SLABS - 1, SLABS)
    my_x, my_z = lax.div(me, 16), lax.rem(me, 16)
    my_half, my_mode = lax.rem(me, 2), lax.div(me, 2)
    own = pl.ds(PLANES, PLANES)

    loads = [
        pltpu.make_async_copy(cot, gbuf.at[own], local_sem.at[0]),
        pltpu.make_async_copy(tst, tbuf.at[own], local_sem.at[1]),
        pltpu.make_async_copy(outer_hbm, outer_ref, local_sem.at[2]),
        pltpu.make_async_copy(inner_hbm, inner_ref, local_sem.at[3]),
        pltpu.make_async_copy(inner_t_hbm, inner_t_ref, local_sem.at[4]),
        pltpu.make_async_copy(outer_t_hbm, outer_t_ref, local_sem.at[5]),
        pltpu.make_async_copy(
            src.at[pl.ds(pl.multiple_of(me * CELLS, CELLS), CELLS)],
            src_recv.at[my_half, my_mode],
            local_sem.at[6],
        ),
        pltpu.make_async_copy(cou_hbm, cou, local_sem.at[9]),
        pltpu.make_async_copy(cod_hbm, cod, local_sem.at[10]),
        pltpu.make_async_copy(strain_hbm, strain, local_sem.at[11]),
        pltpu.make_async_copy(ratio_hbm, ratio_ref, local_sem.at[12]),
        pltpu.make_async_copy(points_hbm, points_ref, local_sem.at[13]),
        pltpu.make_async_copy(moments_hbm, moments_ref, local_sem.at[14]),
    ]
    barrier = pltpu.get_barrier_semaphore()

    def greet(off, _):
        pl.semaphore_signal(
            barrier, inc=1, device_id={"coef": lax.rem(me + off, OWNERS)}, device_id_type=MESH
        )
        return 0

    pl.semaphore_signal(barrier, inc=1, device_id={"slab": above}, device_id_type=MESH)
    pl.semaphore_signal(barrier, inc=1, device_id={"slab": below}, device_id_type=MESH)
    lax.fori_loop(1, OWNERS, greet, 0)
    for n in (7, 8, 9, 0, 1, 6, 11, 2, 3, 4, 5, 10, 12):
        loads[n].start()
    loads[7].wait()
    loads[8].wait()
    scbuf[1] = jnp.where(cod[...] == 1, -cou[...], cou[...])
    pl.semaphore_wait(barrier, OWNERS + 1)

    def halo_copy(way, kind, part):
        target, place = ((above, 0), (below, 2))[way]
        if kind == 0:
            source, dest, sem = scbuf.at[1], scbuf.at[place], 0
        else:
            rows = pl.ds(pl.multiple_of(part * 32, 32), 32)
            planes = pl.ds(place * PLANES, PLANES)
            held, buf = ((tst, tbuf), (cot, gbuf))[kind - 1]
            source, dest, sem = held.at[:, rows], buf.at[planes, rows], 4 * kind - 3 + part
        return pltpu.make_async_remote_copy(
            src_ref=source,
            dst_ref=dest,
            send_sem=halo_send.at[way, sem],
            recv_sem=halo_recv.at[way, sem],
            device_id={"slab": target},
            device_id_type=MESH,
        )

    first_part = lax.div(lax.rem(me, 8), 2)
    order = [lax.rem(first_part + n, 4) for n in (0, 1, 3, 2)]
    for way in range(2):
        halo_copy(way, 0, 0).start()
    for part in order:
        for kind in (1, 2):
            for way in range(2):
                halo_copy(way, kind, part).start()

    loads[9].wait()
    loads[11].wait()
    column_buf[...] = jnp.zeros((128, 128), f32)
    column_buf[0:9, 0:16] = strain[...]
    strain_turned = jnp.transpose(column_buf[...])[0:16]
    col = [strain_turned[:, p : p + 1] for p in range(9)]
    pts = [points_ref[n : n + 1] for n in range(5)]
    line_buf[...] = (col[1] + col[3]) * pts[0] + (col[2] + col[6]) * pts[1]
    square_buf[...] = col[4] * pts[2] + (col[5] + col[7]) * pts[3] + col[8] * pts[4]

    loads[0].wait()
    loads[1].wait()
    for way in range(2):
        halo_copy(way, 0, 0).wait()
    signed = jnp.concatenate([scbuf[0], scbuf[1], scbuf[2], jnp.zeros((116, 128), f32)], axis=0)
    sct_buf[...] = jnp.transpose(signed)
    ones = jnp.ones((8, WIDTH), bf16)

    def chunk(part):
        mu_parts, acc_parts = [], []
        for h in range(2):
            y = pl.multiple_of(part * 16 + h * 8, 8)
            sct = sct_buf[pl.ds(y, 8), :]
            wide = [jnp.broadcast_to(sct[:, p : p + 1], (8, WIDTH)) for p in range(12)]
            upper = [c < 0.0 for c in wide]
            c0 = [jnp.maximum(c, 0.0) for c in wide]
            c1 = [jnp.maximum(-c, 0.0) for c in wide]
            speed = [jnp.abs(c) for c in wide]
            s0 = [
                tbuf[p, pl.ds(pl.multiple_of(part * 16, 16), 16), :].astype(f32)[h * 8 : h * 8 + 8]
                for p in range(12)
            ]
            s = dict(enumerate(s0))
            own_change = []
            for n in range(4):
                edge = {p: s[p + 1] - s[p] for p in range(n, 11 - n)}
                change = {p: jnp.where(upper[p], edge[p], edge[p - 1]) for p in range(n + 1, 11 - n)}
                own_change.append([change[p] for p in range(4, 8)])
                if n < 3:
                    s = {p: s0[p] - section_weights[n] * speed[p] * change[p] for p in change}
            g = {p: gbuf[p, pl.ds(y, 8), :] for p in range(12)}
            mu = [g[p] for p in range(4, 8)]
            acc = [None] * 4
            for k, n in enumerate((3, 2, 1, 0)):
                for p in range(4):
                    term = section_weights[n] * (g[p + 4] * own_change[n][p])
                    acc[p] = term if acc[p] is None else acc[p] + term
                flow = {p: c1[p] * g[p] + c0[p + 1] * g[p + 1] for p in range(k, 11 - k)}
                g = {p: section_weights[n] * (flow[p] - flow[p - 1]) for p in range(k + 1, 11 - k)}
                mu = [mu[p] + g[p + 4] for p in range(4)]
            mu_parts.append(mu)
            acc_parts.append(acc)
        stack = jnp.concatenate([acc_parts[h][p] for p in range(4) for h in range(2)], axis=0)
        total = None
        for piece in halves(stack):
            term = lax.dot_general(
                ones, piece, (((1,), (1,)), ((), ())), preferred_element_type=f32
            )
            total = term if total is None else total + term
        codes = sum_code(total[0:1, :])
        for p in range(4):
            dest = p * 8 + part
            word, level = encode(mu_parts[0][p], mu_parts[1][p])
            mu_send[dest, 0:8, :] = word
            mu_send[dest, 8:9, :] = level
            mu_send[dest, 9:10, 0 : 4 * CELLS] = codes
            where_to = mu_recv.at[my_half, my_mode]

            @pl.when(dest != me)
            def _():
                pltpu.make_async_remote_copy(
                    src_ref=mu_send.at[dest],
                    dst_ref=where_to,
                    send_sem=all_send.at[1],
                    recv_sem=all_recv.at[1],
                    device_id={"coef": dest},
                    device_id_type=MESH,
                ).start()

            @pl.when(dest == me)
            def _():
                pltpu.make_async_copy(mu_send.at[dest], where_to, local_sem.at[7]).start()

    def chunks(step, _):
        part = lax.rem(first_part + step + lax.div(step, 2) * (5 - 2 * step), 4)
        for kind in (1, 2):
            for way in range(2):
                halo_copy(way, kind, part).wait()

        def half(n, _):
            chunk(part * 2 + n)
            return 0

        lax.fori_loop(0, 2, half, 0)
        return 0

    lax.fori_loop(0, 4, chunks, 0)

    def send_source(off, _):
        dest = lax.rem(me + off, OWNERS)
        pltpu.make_async_remote_copy(
            src_ref=src.at[pl.ds(pl.multiple_of(dest * CELLS, CELLS), CELLS)],
            dst_ref=src_recv.at[my_half, my_mode],
            send_sem=all_send.at[0],
            recv_sem=all_recv.at[0],
            device_id={"coef": dest},
            device_id_type=MESH,
        ).start()
        return 0

    lax.fori_loop(1, OWNERS, send_source, 0)

    def wait_all(ref, sem):
        pltpu.make_async_copy(ref, ref, sem).wait()

    src_31 = src.at[pl.ds(0, (OWNERS - 1) * CELLS)]
    for n in (2, 3, 4, 5, 6, 10, 12):
        loads[n].wait()
    outer = (outer_ref[0], outer_ref[1])
    inner = (inner_ref[0], inner_ref[1])

    wait_all(mu_send.at[pl.ds(0, OWNERS - 1)], all_recv.at[1])
    pltpu.make_async_copy(mu_send.at[0], mu_send.at[0], local_sem.at[7]).wait()
    mu_high, mu_low = [], []
    for half in range(2):
        high_rows, low_rows = [], []
        for mode in range(NH):
            block = jnp.concatenate(
                decode(
                    mu_recv[half, mode, 0:8, :], mu_recv[half, mode, 8:9, :], weight_cube
                ),
                axis=0,
            )
            high, low = halves(block)
            high_rows.append(high)
            low_rows.append(low)
        mu_high.append(jnp.concatenate(high_rows, axis=0))
        mu_low.append(jnp.concatenate(low_rows, axis=0))
    mu_cells = (jnp.concatenate(mu_high, axis=1), jnp.concatenate(mu_low, axis=1))
    first = halves(product(outer, mu_cells))
    inner_t = (inner_t_ref[0], inner_t_ref[1])
    outer_t = (outer_t_ref[0], outer_t_ref[1])
    line, square = line_buf[...], square_buf[...]
    back = []
    for block in range(3):
        here = slice(block * 128, block * 128 + 128)
        values = product((first[0][here], first[1][here]), inner)
        u_buf[here, :] = values
        weighted = []
        for n in range(8):
            a = block * 8 + n
            u = values[n * CELLS : n * CELLS + CELLS]
            x = float(nodes[a])
            form = (square + x * (line + x * col[0])) * ratio_ref[a : a + 1, :]
            weighted.append(u + u * form)
        back.append(product(halves(jnp.concatenate(weighted, axis=0)), inner_t))
    adj = product(outer_t, halves(jnp.concatenate(back, axis=0)))
    for mode in range(NH):
        for half in range(2):
            dest = 2 * mode + half
            block = adj[mode * CELLS : mode * CELLS + CELLS, half * WIDTH : half * WIDTH + WIDTH]
            word, level = encode(block[0:8], block[8:16])
            back_send[dest, 0:8, :] = word
            back_send[dest, 8:9, :] = level

    def send_back(step, _):
        z = lax.div(step, 2)
        late = z - 8
        z = jnp.where(z < 8, z, jnp.where(z < 12, 15 - late, late + 4))
        dest = lax.rem(step, 2) * 16 + z

        @pl.when(dest != me)
        def _():
            pltpu.make_async_remote_copy(
                src_ref=back_send.at[dest],
                dst_ref=back_recv.at[me],
                send_sem=all_send.at[3],
                recv_sem=all_recv.at[3],
                device_id={"coef": dest},
                device_id_type=MESH,
            ).start()

        return 0

    lax.fori_loop(0, OWNERS, send_back, 0)
    own_back = pltpu.make_async_copy(back_send.at[me], back_recv.at[me], local_sem.at[8])
    own_back.start()

    total = None
    for half in range(2):
        for mode in range(NH):
            row = sum_value(mu_recv[half, mode, 9:10, 0 : 4 * CELLS])
            total = row if total is None else total + row
    courant_buf[...] = jnp.zeros((8, 128), f32)
    courant_buf[0:1, 0 : 4 * CELLS] = total
    turn = lax.rem(128 - lax.div(me, 8) * CELLS, 128)
    turned = pltpu.roll(courant_buf[...], turn, 1) * (-1.0 / math.sqrt(K))
    courant_out[...] = turned[0:1, 0:CELLS]
    outs = [pltpu.make_async_copy(courant_out, out_courant, local_sem.at[15])]
    outs[0].start()

    wait_all(src_31, all_recv.at[0])
    source = jnp.concatenate(
        [src_recv[0].reshape(256, WIDTH), src_recv[1].reshape(256, WIDTH)], axis=1
    )
    es_buf[...] = product(halves(product(outer, (source,))), inner)
    sums = [None, None, None]
    for a in range(QP):
        here = slice(a * CELLS, a * CELLS + CELLS)
        y = u_buf[here, :] * es_buf[here, :] * ratio_ref[a : a + 1, :]
        x = float(nodes[a])
        for n, term in enumerate((y, x * y, (x * x) * y)):
            sums[n] = term if sums[n] is None else sums[n] + term
    strain_sum = None
    for n in range(3):
        part = lax.dot_general(
            moments_ref[n],
            sums[n],
            (((1,), (1,)), ((), ())),
            precision=lax.Precision.HIGHEST,
            preferred_element_type=f32,
        )
        strain_sum = part if strain_sum is None else strain_sum + part
    strain_buf[...] = strain_sum[0:9, :]
    outs.append(pltpu.make_async_copy(strain_buf, out_strain, local_sem.at[16]))
    outs[1].start()

    own_back.wait()
    for copy in outs:
        copy.wait()
    wait_all(src_31, all_send.at[0])
    wait_all(mu_send.at[pl.ds(0, OWNERS - 1)], all_send.at[1])
    wait_all(back_send.at[pl.ds(0, OWNERS - 1)], all_send.at[3])
    wait_all(back_send.at[pl.ds(0, OWNERS - 1)], all_recv.at[3])


def finish(
    back_hbm, strain_hbm, courant_hbm, out_source, out_strain, out_courant, back, source, sem
):
    small = [
        pltpu.make_async_copy(strain_hbm, out_strain, sem.at[0]),
        pltpu.make_async_copy(courant_hbm, out_courant, sem.at[1]),
    ]
    load = pltpu.make_async_copy(back_hbm, back, sem.at[2])
    load.start()
    for copy in small:
        copy.start()
    load.wait()
    stores = []
    for part in range(2):
        for n in range(part * 16, part * 16 + 16):
            low, high = decode(back[n, 0:8, :], back[n, 8:9, :], 1.0)
            source[n * CELLS : n * CELLS + 8, :] = low
            source[n * CELLS + 8 : n * CELLS + 16, :] = high
        here = pl.ds(part * 256, 256)
        stores.append(pltpu.make_async_copy(source.at[here], out_source.at[here], sem.at[3 + part]))
        stores[-1].start()
    for copy in small + stores:
        copy.wait()


def body(cotangent, transport_state, source_state, courant, upwind_codes, strain_rate):
    nodes, *constants = tables()
    rows = PLANES * CYZ
    hbm = pl.BlockSpec(memory_space=pltpu.HBM)
    results = pl.pallas_call(
        functools.partial(kernel, nodes),
        out_shape=(
            jax.ShapeDtypeStruct((OWNERS, 9, WIDTH), jnp.int32),
            jax.ShapeDtypeStruct((9, CELLS), f32),
            jax.ShapeDtypeStruct((1, CELLS), f32),
        ),
        in_specs=[hbm] * 13,
        out_specs=[hbm] * 3,
        scratch_shapes=[
            pltpu.VMEM((3 * PLANES, CYZ, WIDTH), f32),
            pltpu.VMEM((3 * PLANES, CYZ, WIDTH), bf16),
            pltpu.VMEM((3, PLANES, CYZ), f32),
            pltpu.VMEM((128, 128), f32),
            pltpu.VMEM((2, NH, CELLS, WIDTH), bf16),
            pltpu.VMEM((OWNERS, 10, WIDTH), jnp.int32),
            pltpu.VMEM((2, NH, 10, WIDTH), jnp.int32),
            pltpu.VMEM((OWNERS, 9, WIDTH), jnp.int32),
            pltpu.VMEM((PLANES, CYZ), f32),
            pltpu.VMEM((PLANES, CYZ), jnp.int32),
            pltpu.VMEM((9, CELLS), f32),
            pltpu.VMEM((2, QP * CELLS, NH * CELLS), bf16),
            pltpu.VMEM((2, NH * NH, POINTS), bf16),
            pltpu.VMEM((2, POINTS, NH * NH), bf16),
            pltpu.VMEM((2, NH * CELLS, QP * CELLS), bf16),
            pltpu.VMEM((QP, POINTS), f32),
            pltpu.VMEM((8, POINTS), f32),
            pltpu.VMEM((3, 16, POINTS), f32),
            pltpu.VMEM((QP * CELLS, POINTS), f32),
            pltpu.VMEM((QP * CELLS, POINTS), f32),
            pltpu.VMEM((CELLS, POINTS), f32),
            pltpu.VMEM((CELLS, POINTS), f32),
            pltpu.VMEM((128, 128), f32),
            pltpu.VMEM((9, CELLS), f32),
            pltpu.VMEM((8, WIDTH), f32),
            pltpu.VMEM((1, CELLS), f32),
            pltpu.SemaphoreType.DMA((17,)),
            pltpu.SemaphoreType.DMA((2, 9)),
            pltpu.SemaphoreType.DMA((2, 9)),
            pltpu.SemaphoreType.DMA((4,)),
            pltpu.SemaphoreType.DMA((4,)),
        ],
        compiler_params=pltpu.CompilerParams(
            collective_id=0, has_side_effects=True, vmem_limit_bytes=60 * 2**20
        ),
    )(
        cotangent.reshape(PLANES, CYZ, WIDTH),
        transport_state.reshape(PLANES, CYZ, WIDTH),
        source_state,
        courant.reshape(PLANES, CYZ),
        upwind_codes.reshape(PLANES, CYZ),
        strain_rate,
        *[jnp.asarray(table) for table in constants],
    )
    adj_source, adj_strain, adj_courant = pl.pallas_call(
        finish,
        out_shape=(
            jax.ShapeDtypeStruct((rows, WIDTH), f32),
            jax.ShapeDtypeStruct((9, CELLS), f32),
            jax.ShapeDtypeStruct((1, CELLS), f32),
        ),
        in_specs=[hbm] * 3,
        out_specs=[hbm] * 3,
        scratch_shapes=[
            pltpu.VMEM((OWNERS, 9, WIDTH), jnp.int32),
            pltpu.VMEM((rows, WIDTH), f32),
            pltpu.SemaphoreType.DMA((5,)),
        ],
        compiler_params=pltpu.CompilerParams(vmem_limit_bytes=60 * 2**20),
    )(*results)
    return adj_source, adj_strain, adj_courant.reshape(CELLS)


def solution(mesh):
    placed = (
        P("slab", "coef"),
        P("slab", "coef"),
        P("slab", "coef"),
        P("slab"),
        P("slab"),
        P(None, ("slab", "coef")),
    )
    return jax.shard_map(
        body,
        mesh=mesh,
        in_specs=placed,
        out_specs=(P("slab", "coef"), P(None, ("slab", "coef")), P(("slab", "coef"))),
        check_vma=False,
    )
```

time: 64.3 us -> 48.5 us (0.75)
  the two profiles are of different devices: /device:TPU:2 before, /device:TPU:64 now
where the time goes in v2:
time: 48.5 us; the launch traced here: 48.3 us
  Pallas kernels  47.7 us (98%)
  between operations  0.64 us (1%)
    pallas_call x1, Pallas kernels, body(): pl.pallas_call(functools.partial(kernel, nodes), out_shape=(jax.ShapeDtyp...  46 us
    pallas_call x1, Pallas kernels, body(): pl.pallas_call(finish, out_shape=(jax.ShapeDtypeStruct((rows, WIDTH), f32...  1.68 us

profile of v2, /device:TPU:64, one launch (start us, length us, event | category | flops | bytes accessed | tf_op | source)
XLA Modules:
  0.0 48.3 jit_solution(508891415800727361)
XLA Ops:
  0.6 46.0 %shard_map.148 = (s32[32,9,128]{2,1,0:T(8,128)}, f32[9,16]{1,0:T(8,128)}, f32[1,16]{1,0:T(1,128)}) custom-call(f32[4,128,128]{2,1,0:T(8,128)} %bitcast.5, bf16[4,128,128]{2,1,0:T(8,128)(2,1)} %bitcast.6, bf16[512,128]{1,0:T(8,128)(2,1)} %src.1, f32[4,128]{1,0:T(4,128)} %bitcast.7, s32[4,128]{1,0:T(4,128)} %bitcast.8, f32[9,16]{1,0:T(8,128)} %strain_hbm.1, ...), custom_call_target="tpu_custom_call" | custom-call | tf_op jit(solution)/shard_map/pallas_call | solution.py:470
  46.6 1.7 %shard_map.149 = (f32[512,128]{1,0:T(8,128)}, f32[9,16]{1,0:T(8,128)}, f32[1,16]{1,0:T(1,128)}) custom-call(s32[32,9,128]{2,1,0:T(8,128)} %get-tuple-element.9.back_hbm, f32[9,16]{1,0:T(8,128)} %get-tuple-element.10.strain_hbm, f32[1,16]{1,0:T(1,128)} %get-tuple-element.11.courant_hbm), custom_call_target="tpu_custom_call" | custom-call | tf_op jit(solution)/shard_map/pallas_call | solution.py:524

commit v3 on v2

--- a/solution.py
+++ b/solution.py
@@ -30,6 +30,10 @@
 f32 = jnp.float32
 bf16 = jnp.bfloat16
 MESH = pl.DeviceIdType.MESH
+
+away_order = (8, 7, -7, 6, -6, 5, -5, 4, -4, 3, -3, 2, -2, 1, -1, 0)
+far = [(away, other) for away in away_order[:7] for other in (1, 0)]
+near = [(away, other) for away in away_order[7:] for other in (1, 0) if (away, other) != (0, 0)]
 
 
 def split_table(table):
@@ -123,12 +127,12 @@
     cot, tst, src, cou_hbm, cod_hbm, strain_hbm,
     outer_hbm, inner_hbm, inner_t_hbm, outer_t_hbm, ratio_hbm, points_hbm, moments_hbm,
     back_recv, out_strain, out_courant,
-    gbuf, tbuf, scbuf, sct_buf,
+    gbuf, tbuf, scbuf, sct_buf, code_send, code_recv,
     src_recv, mu_send, mu_recv, back_send,
     cou, cod, strain,
     outer_ref, inner_ref, inner_t_ref, outer_t_ref, ratio_ref, points_ref, moments_ref,
     u_buf, es_buf, square_buf, line_buf, column_buf, strain_buf, courant_buf, courant_out,
-    local_sem, halo_send, halo_recv, all_send, all_recv,
+    local_sem, halo_send, halo_recv, all_send, all_recv, near_sem,
 ):
     me = lax.axis_index("coef")
     slab = lax.axis_index("slab")
@@ -139,7 +143,7 @@
     own = pl.ds(PLANES, PLANES)
 
     loads = [
-        pltpu.make_async_copy(cot, gbuf.at[own], local_sem.at[0]),
+        pltpu.make_async_copy(cot, gbuf, local_sem.at[0]),
         pltpu.make_async_copy(tst, tbuf.at[own], local_sem.at[1]),
         pltpu.make_async_copy(outer_hbm, outer_ref, local_sem.at[2]),
         pltpu.make_async_copy(inner_hbm, inner_ref, local_sem.at[3]),
@@ -159,31 +163,44 @@
     ]
     barrier = pltpu.get_barrier_semaphore()
 
-    def greet(off, _):
-        pl.semaphore_signal(
-            barrier, inc=1, device_id={"coef": lax.rem(me + off, OWNERS)}, device_id_type=MESH
-        )
-        return 0
+    def owner(away, other):
+        return lax.rem(my_x + other, 2) * 16 + lax.rem(my_z + away + 16, 16)
+
+    def signal_near(sem):
+        for away, other in near:
+            pl.semaphore_signal(
+                sem, inc=1, device_id={"coef": owner(away, other)}, device_id_type=MESH
+            )
 
     pl.semaphore_signal(barrier, inc=1, device_id={"slab": above}, device_id_type=MESH)
     pl.semaphore_signal(barrier, inc=1, device_id={"slab": below}, device_id_type=MESH)
-    lax.fori_loop(1, OWNERS, greet, 0)
-    for n in (7, 8, 9, 0, 1, 6, 11, 2, 3, 4, 5, 10, 12):
+    signal_near(barrier)
+    for n in (0, 7, 8, 9, 1, 6, 11, 2, 3, 4, 5, 10, 12):
         loads[n].start()
     loads[7].wait()
     loads[8].wait()
     scbuf[1] = jnp.where(cod[...] == 1, -cou[...], cou[...])
-    pl.semaphore_wait(barrier, OWNERS + 1)
+    loads[0].wait()
+    for part in range(4):
+        for p in range(PLANES):
+            for n in range(2):
+                y = part * 32 + n * 16
+                word, level = encode(gbuf[p, y : y + 8, :], gbuf[p, y + 8 : y + 16, :])
+                code_send[part, p * 2 + n, 0:8, :] = word
+                code_send[part, p * 2 + n, 8:9, :] = level
+    pl.semaphore_wait(barrier, len(near) + 2)
+    signal_near(near_sem)
 
     def halo_copy(way, kind, part):
         target, place = ((above, 0), (below, 2))[way]
         if kind == 0:
             source, dest, sem = scbuf.at[1], scbuf.at[place], 0
-        else:
+        elif kind == 1:
             rows = pl.ds(pl.multiple_of(part * 32, 32), 32)
             planes = pl.ds(place * PLANES, PLANES)
-            held, buf = ((tst, tbuf), (cot, gbuf))[kind - 1]
-            source, dest, sem = held.at[:, rows], buf.at[planes, rows], 4 * kind - 3 + part
+            source, dest, sem = tst.at[:, rows], tbuf.at[planes, rows], 1 + part
+        else:
+            source, dest, sem = code_send.at[part], code_recv.at[way, part], 5 + part
         return pltpu.make_async_remote_copy(
             src_ref=source,
             dst_ref=dest,
@@ -201,6 +218,20 @@
         for kind in (1, 2):
             for way in range(2):
                 halo_copy(way, kind, part).start()
+
+    def send_source(away, other):
+        dest = owner(away, other)
+        pltpu.make_async_remote_copy(
+            src_ref=src.at[pl.ds(pl.multiple_of(dest * CELLS, CELLS), CELLS)],
+            dst_ref=src_recv.at[my_half, my_mode],
+            send_sem=all_send.at[0],
+            recv_sem=all_recv.at[0],
+            device_id={"coef": dest},
+            device_id_type=MESH,
+        ).start()
+
+    for away, other in near:
+        send_source(away, other)
 
     loads[9].wait()
     loads[11].wait()
@@ -212,7 +243,6 @@
     line_buf[...] = (col[1] + col[3]) * pts[0] + (col[2] + col[6]) * pts[1]
     square_buf[...] = col[4] * pts[2] + (col[5] + col[7]) * pts[3] + col[8] * pts[4]
 
-    loads[0].wait()
     loads[1].wait()
     for way in range(2):
         halo_copy(way, 0, 0).wait()
@@ -220,8 +250,15 @@
     sct_buf[...] = jnp.transpose(signed)
     ones = jnp.ones((8, WIDTH), bf16)
 
-    def chunk(part):
+    def chunk(quarter, n):
+        part = quarter * 2 + n
         mu_parts, acc_parts = [], []
+        coded = [
+            (code_recv.at[way, quarter, p * 2 + n], way * 8 + p)
+            for way in range(2)
+            for p in range(PLANES)
+        ]
+        unit = {p: jnp.exp2(ref[8:9, :].astype(f32) * 0.125) * (1.0 / code_top) for ref, p in coded}
         for h in range(2):
             y = pl.multiple_of(part * 16 + h * 8, 8)
             sct = sct_buf[pl.ds(y, 8), :]
@@ -242,7 +279,12 @@
                 own_change.append([change[p] for p in range(4, 8)])
                 if n < 3:
                     s = {p: s0[p] - section_weights[n] * speed[p] * change[p] for p in change}
-            g = {p: gbuf[p, pl.ds(y, 8), :] for p in range(12)}
+            g = {p + 4: gbuf[p, pl.ds(y, 8), :] for p in range(PLANES)}
+            for ref, p in coded:
+                word = ref[0:8, :]
+                if h == 0:
+                    word = lax.shift_left(word, 16)
+                g[p] = lax.shift_right_arithmetic(word, 16).astype(f32) * unit[p]
             mu = [g[p] for p in range(4, 8)]
             acc = [None] * 4
             for k, n in enumerate((3, 2, 1, 0)):
@@ -292,27 +334,20 @@
                 halo_copy(way, kind, part).wait()
 
         def half(n, _):
-            chunk(part * 2 + n)
+            chunk(part, n)
             return 0
+
+        @pl.when(step == 0)
+        def _():
+            pl.semaphore_wait(near_sem, len(near))
 
         lax.fori_loop(0, 2, half, 0)
         return 0
 
     lax.fori_loop(0, 4, chunks, 0)
 
-    def send_source(off, _):
-        dest = lax.rem(me + off, OWNERS)
-        pltpu.make_async_remote_copy(
-            src_ref=src.at[pl.ds(pl.multiple_of(dest * CELLS, CELLS), CELLS)],
-            dst_ref=src_recv.at[my_half, my_mode],
-            send_sem=all_send.at[0],
-            recv_sem=all_recv.at[0],
-            device_id={"coef": dest},
-            device_id_type=MESH,
-        ).start()
-        return 0
-
-    lax.fori_loop(1, OWNERS, send_source, 0)
+    for away, other in far:
+        send_source(away, other)
 
     def wait_all(ref, sem):
         pltpu.make_async_copy(ref, ref, sem).wait()
@@ -445,19 +480,21 @@
         pltpu.make_async_copy(strain_hbm, out_strain, sem.at[0]),
         pltpu.make_async_copy(courant_hbm, out_courant, sem.at[1]),
     ]
-    load = pltpu.make_async_copy(back_hbm, back, sem.at[2])
-    load.start()
-    for copy in small:
+    loads = [
+        pltpu.make_async_copy(back_hbm.at[here], back.at[here], sem.at[2 + part])
+        for part, here in enumerate(pl.ds(n * 8, 8) for n in range(4))
+    ]
+    for copy in loads + small:
         copy.start()
-    load.wait()
     stores = []
-    for part in range(2):
-        for n in range(part * 16, part * 16 + 16):
+    for part in range(4):
+        loads[part].wait()
+        for n in range(part * 8, part * 8 + 8):
             low, high = decode(back[n, 0:8, :], back[n, 8:9, :], 1.0)
             source[n * CELLS : n * CELLS + 8, :] = low
             source[n * CELLS + 8 : n * CELLS + 16, :] = high
-        here = pl.ds(part * 256, 256)
-        stores.append(pltpu.make_async_copy(source.at[here], out_source.at[here], sem.at[3 + part]))
+        here = pl.ds(part * 128, 128)
+        stores.append(pltpu.make_async_copy(source.at[here], out_source.at[here], sem.at[6 + part]))
         stores[-1].start()
     for copy in small + stores:
         copy.wait()
@@ -477,10 +514,12 @@
         in_specs=[hbm] * 13,
         out_specs=[hbm] * 3,
         scratch_shapes=[
-            pltpu.VMEM((3 * PLANES, CYZ, WIDTH), f32),
+            pltpu.VMEM((PLANES, CYZ, WIDTH), f32),
             pltpu.VMEM((3 * PLANES, CYZ, WIDTH), bf16),
             pltpu.VMEM((3, PLANES, CYZ), f32),
             pltpu.VMEM((128, 128), f32),
+            pltpu.VMEM((4, 2 * PLANES, 9, WIDTH), jnp.int32),
+            pltpu.VMEM((2, 4, 2 * PLANES, 9, WIDTH), jnp.int32),
             pltpu.VMEM((2, NH, CELLS, WIDTH), bf16),
             pltpu.VMEM((OWNERS, 10, WIDTH), jnp.int32),
             pltpu.VMEM((2, NH, 10, WIDTH), jnp.int32),
@@ -508,6 +547,7 @@
             pltpu.SemaphoreType.DMA((2, 9)),
             pltpu.SemaphoreType.DMA((4,)),
             pltpu.SemaphoreType.DMA((4,)),
+            pltpu.SemaphoreType.REGULAR,
         ],
         compiler_params=pltpu.CompilerParams(
             collective_id=0, has_side_effects=True, vmem_limit_bytes=60 * 2**20
@@ -533,7 +573,7 @@
         scratch_shapes=[
             pltpu.VMEM((OWNERS, 9, WIDTH), jnp.int32),
             pltpu.VMEM((rows, WIDTH), f32),
-            pltpu.SemaphoreType.DMA((5,)),
+            pltpu.SemaphoreType.DMA((10,)),
         ],
         compiler_params=pltpu.CompilerParams(vmem_limit_bytes=60 * 2**20),
     )(*results)

time: 48.5 us -> 46.9 us (0.967)
  the two profiles are of different devices: /device:TPU:64 before, /device:TPU:2 now
where the time goes in v3:
time: 46.9 us; the launch traced here: 46.7 us
  Pallas kernels  46.1 us (98%)
  between operations  0.64 us (1%)
    pallas_call x1, Pallas kernels, body(): pl.pallas_call(functools.partial(kernel, nodes), out_shape=(jax.ShapeDtyp...  44.5 us
    pallas_call x1, Pallas kernels, body(): pl.pallas_call(finish, out_shape=(jax.ShapeDtypeStruct((rows, WIDTH), f32...  1.57 us

profile of v3, /device:TPU:2, one launch (start us, length us, event | category | flops | bytes accessed | tf_op | source)
XLA Modules:
  0.0 46.7 jit_solution(12409429924426926119)
XLA Ops:
  0.6 44.5 %shard_map.148 = (s32[32,9,128]{2,1,0:T(8,128)}, f32[9,16]{1,0:T(8,128)}, f32[1,16]{1,0:T(1,128)}) custom-call(f32[4,128,128]{2,1,0:T(8,128)} %bitcast.5, bf16[4,128,128]{2,1,0:T(8,128)(2,1)} %bitcast.6, bf16[512,128]{1,0:T(8,128)(2,1)} %src.1, f32[4,128]{1,0:T(4,128)} %bitcast.7, s32[4,128]{1,0:T(4,128)} %bitcast.8, f32[9,16]{1,0:T(8,128)} %strain_hbm.1, ...), custom_call_target="tpu_custom_call" | custom-call | tf_op jit(solution)/shard_map/pallas_call | solution.py:507
  45.1 1.6 %shard_map.149 = (f32[512,128]{1,0:T(8,128)}, f32[9,16]{1,0:T(8,128)}, f32[1,16]{1,0:T(1,128)}) custom-call(s32[32,9,128]{2,1,0:T(8,128)} %get-tuple-element.9.back_hbm, f32[9,16]{1,0:T(8,128)} %get-tuple-element.10.strain_hbm, f32[1,16]{1,0:T(1,128)} %get-tuple-element.11.courant_hbm), custom_call_target="tpu_custom_call" | custom-call | tf_op jit(solution)/shard_map/pallas_call | solution.py:564

commit v4 on v3

--- a/solution.py
+++ b/solution.py
@@ -31,6 +31,7 @@
 bf16 = jnp.bfloat16
 MESH = pl.DeviceIdType.MESH
 
+next_owners = [(1, 0), (-1, 0), (0, 1), (1, 1), (-1, 1)]
 away_order = (8, 7, -7, 6, -6, 5, -5, 4, -4, 3, -3, 2, -2, 1, -1, 0)
 far = [(away, other) for away in away_order[:7] for other in (1, 0)]
 near = [(away, other) for away in away_order[7:] for other in (1, 0) if (away, other) != (0, 0)]
@@ -94,8 +95,8 @@
 
 def encode(low, high):
     top = jnp.max(jnp.maximum(jnp.abs(low), jnp.abs(high)), axis=0, keepdims=True)
-    level = jnp.ceil(jnp.log2(jnp.maximum(top, 1e-30)) * 8.0)
-    unit = jnp.exp2(level * -0.125) * code_top
+    level = jnp.ceil(jnp.log2(jnp.maximum(top, 1e-30)) * 2.0)
+    unit = jnp.exp2(level * -0.5) * code_top
     low_code = jnp.round(low * unit).astype(jnp.int32)
     high_code = jnp.round(high * unit).astype(jnp.int32)
     word = jnp.bitwise_or(lax.shift_left(high_code, 16), jnp.bitwise_and(low_code, 0xFFFF))
@@ -103,7 +104,7 @@
 
 
 def decode(word, level, factor):
-    unit = jnp.exp2(level.astype(f32) * 0.125) * (factor / code_top)
+    unit = jnp.exp2(level.astype(f32) * 0.5) * (factor / code_top)
     low = lax.shift_right_arithmetic(lax.shift_left(word, 16), 16).astype(f32) * unit
     high = lax.shift_right_arithmetic(word, 16).astype(f32) * unit
     return low, high
@@ -111,13 +112,13 @@
 
 def sum_code(value):
     size = jnp.abs(value)
-    code = jnp.round((jnp.log2(jnp.maximum(size, 1e-30)) + 100.0) * 2.0**20).astype(jnp.int32)
+    code = jnp.round((jnp.log2(jnp.maximum(size, 1e-30)) + 100.0) * 2.0**16).astype(jnp.int32)
     code = jnp.where(size < 1e-30, 0, code)
     return jnp.where(value < 0.0, -code, code)
 
 
 def sum_value(code):
-    size = jnp.exp2(jnp.abs(code).astype(f32) * 2.0**-20 - 100.0)
+    size = jnp.exp2(jnp.abs(code).astype(f32) * 2.0**-16 - 100.0)
     size = jnp.where(code == 0, 0.0, size)
     return jnp.where(code < 0, -size, size)
 
@@ -132,7 +133,7 @@
     cou, cod, strain,
     outer_ref, inner_ref, inner_t_ref, outer_t_ref, ratio_ref, points_ref, moments_ref,
     u_buf, es_buf, square_buf, line_buf, column_buf, strain_buf, courant_buf, courant_out,
-    local_sem, halo_send, halo_recv, all_send, all_recv, near_sem,
+    local_sem, halo_send, halo_recv, all_send, all_recv, meet_sem,
 ):
     me = lax.axis_index("coef")
     slab = lax.axis_index("slab")
@@ -166,30 +167,21 @@
     def owner(away, other):
         return lax.rem(my_x + other, 2) * 16 + lax.rem(my_z + away + 16, 16)
 
-    def signal_near(sem):
-        for away, other in near:
-            pl.semaphore_signal(
-                sem, inc=1, device_id={"coef": owner(away, other)}, device_id_type=MESH
-            )
+    def signal(sem, away, other):
+        pl.semaphore_signal(
+            sem, inc=1, device_id={"coef": owner(away, other)}, device_id_type=MESH
+        )
 
     pl.semaphore_signal(barrier, inc=1, device_id={"slab": above}, device_id_type=MESH)
     pl.semaphore_signal(barrier, inc=1, device_id={"slab": below}, device_id_type=MESH)
-    signal_near(barrier)
-    for n in (0, 7, 8, 9, 1, 6, 11, 2, 3, 4, 5, 10, 12):
+    for away, other in next_owners:
+        signal(barrier, away, other)
+    for n in (7, 8, 0, 1, 9, 11):
         loads[n].start()
     loads[7].wait()
     loads[8].wait()
     scbuf[1] = jnp.where(cod[...] == 1, -cou[...], cou[...])
-    loads[0].wait()
-    for part in range(4):
-        for p in range(PLANES):
-            for n in range(2):
-                y = part * 32 + n * 16
-                word, level = encode(gbuf[p, y : y + 8, :], gbuf[p, y + 8 : y + 16, :])
-                code_send[part, p * 2 + n, 0:8, :] = word
-                code_send[part, p * 2 + n, 8:9, :] = level
-    pl.semaphore_wait(barrier, len(near) + 2)
-    signal_near(near_sem)
+    pl.semaphore_wait(barrier, len(next_owners) + 2)
 
     def halo_copy(way, kind, part):
         target, place = ((above, 0), (below, 2))[way]
@@ -214,10 +206,35 @@
     order = [lax.rem(first_part + n, 4) for n in (0, 1, 3, 2)]
     for way in range(2):
         halo_copy(way, 0, 0).start()
-    for part in order:
-        for kind in (1, 2):
+    for way in range(2):
+        halo_copy(way, 1, order[0]).start()
+    loads[0].wait()
+    for step in range(4):
+        for p in range(PLANES):
+            for n in range(2):
+                y = order[step] * 32 + n * 16
+                word, level = encode(
+                    gbuf[p, pl.ds(pl.multiple_of(y, 8), 8), :],
+                    gbuf[p, pl.ds(pl.multiple_of(y + 8, 8), 8), :],
+                )
+                code_send[order[step], p * 2 + n, 0:8, :] = word
+                code_send[order[step], p * 2 + n, 8:9, :] = level
+        for way in range(2):
+            halo_copy(way, 2, order[step]).start()
+        if step < 3:
             for way in range(2):
-                halo_copy(way, kind, part).start()
+                halo_copy(way, 1, order[step + 1]).start()
+    for n in (6, 2, 3, 4, 5, 10, 12):
+        loads[n].start()
+
+    for away, other in next_owners:
+        signal(meet_sem.at[0], away, other)
+    pl.semaphore_wait(meet_sem.at[0], len(next_owners))
+    signal(meet_sem.at[1], 2, 0)
+    signal(meet_sem.at[1], -2, 0)
+    pl.semaphore_wait(meet_sem.at[1], 2)
+    signal(meet_sem.at[2], 4, 0)
+    signal(meet_sem.at[2], -4, 0)
 
     def send_source(away, other):
         dest = owner(away, other)
@@ -230,8 +247,6 @@
             device_id_type=MESH,
         ).start()
 
-    for away, other in near:
-        send_source(away, other)
 
     loads[9].wait()
     loads[11].wait()
@@ -258,7 +273,7 @@
             for way in range(2)
             for p in range(PLANES)
         ]
-        unit = {p: jnp.exp2(ref[8:9, :].astype(f32) * 0.125) * (1.0 / code_top) for ref, p in coded}
+        unit = {p: jnp.exp2(ref[8:9, :].astype(f32) * 0.5) * (1.0 / code_top) for ref, p in coded}
         for h in range(2):
             y = pl.multiple_of(part * 16 + h * 8, 8)
             sct = sct_buf[pl.ds(y, 8), :]
@@ -296,36 +311,23 @@
                 mu = [mu[p] + g[p + 4] for p in range(4)]
             mu_parts.append(mu)
             acc_parts.append(acc)
-        stack = jnp.concatenate([acc_parts[h][p] for p in range(4) for h in range(2)], axis=0)
+        stack = jnp.concatenate(
+            [acc_parts[h][p] for p in range(4) for h in range(2)]
+            + [jnp.zeros((WIDTH - 4 * CELLS, WIDTH), f32)],
+            axis=0,
+        )
         total = None
         for piece in halves(stack):
             term = lax.dot_general(
                 ones, piece, (((1,), (1,)), ((), ())), preferred_element_type=f32
             )
             total = term if total is None else total + term
-        codes = sum_code(total[0:1, :])
+        codes = lax.shift_left(sum_code(total[0:1, :]), 8)
         for p in range(4):
             dest = p * 8 + part
             word, level = encode(mu_parts[0][p], mu_parts[1][p])
             mu_send[dest, 0:8, :] = word
-            mu_send[dest, 8:9, :] = level
-            mu_send[dest, 9:10, 0 : 4 * CELLS] = codes
-            where_to = mu_recv.at[my_half, my_mode]
-
-            @pl.when(dest != me)
-            def _():
-                pltpu.make_async_remote_copy(
-                    src_ref=mu_send.at[dest],
-                    dst_ref=where_to,
-                    send_sem=all_send.at[1],
-                    recv_sem=all_recv.at[1],
-                    device_id={"coef": dest},
-                    device_id_type=MESH,
-                ).start()
-
-            @pl.when(dest == me)
-            def _():
-                pltpu.make_async_copy(mu_send.at[dest], where_to, local_sem.at[7]).start()
+            mu_send[dest, 8:9, :] = jnp.bitwise_or(codes, level + 200)
 
     def chunks(step, _):
         part = lax.rem(first_part + step + lax.div(step, 2) * (5 - 2 * step), 4)
@@ -337,16 +339,27 @@
             chunk(part, n)
             return 0
 
-        @pl.when(step == 0)
-        def _():
-            pl.semaphore_wait(near_sem, len(near))
-
         lax.fori_loop(0, 2, half, 0)
         return 0
 
     lax.fori_loop(0, 4, chunks, 0)
 
+    pl.semaphore_wait(meet_sem.at[2], 2)
+    for away, other in far + near:
+        dest = owner(away, other)
+        pltpu.make_async_remote_copy(
+            src_ref=mu_send.at[dest],
+            dst_ref=mu_recv.at[my_half, my_mode],
+            send_sem=all_send.at[1],
+            recv_sem=all_recv.at[1],
+            device_id={"coef": dest},
+            device_id_type=MESH,
+        ).start()
+    own_mu = pltpu.make_async_copy(mu_send.at[me], mu_recv.at[my_half, my_mode], local_sem.at[7])
+    own_mu.start()
     for away, other in far:
+        send_source(away, other)
+    for away, other in near:
         send_source(away, other)
 
     def wait_all(ref, sem):
@@ -359,14 +372,16 @@
     inner = (inner_ref[0], inner_ref[1])
 
     wait_all(mu_send.at[pl.ds(0, OWNERS - 1)], all_recv.at[1])
-    pltpu.make_async_copy(mu_send.at[0], mu_send.at[0], local_sem.at[7]).wait()
+    own_mu.wait()
     mu_high, mu_low = [], []
     for half in range(2):
         high_rows, low_rows = [], []
         for mode in range(NH):
             block = jnp.concatenate(
                 decode(
-                    mu_recv[half, mode, 0:8, :], mu_recv[half, mode, 8:9, :], weight_cube
+                    mu_recv[half, mode, 0:8, :],
+                    jnp.bitwise_and(mu_recv[half, mode, 8:9, :], 255) - 200,
+                    weight_cube,
                 ),
                 axis=0,
             )
@@ -428,10 +443,9 @@
     total = None
     for half in range(2):
         for mode in range(NH):
-            row = sum_value(mu_recv[half, mode, 9:10, 0 : 4 * CELLS])
+            row = sum_value(lax.shift_right_arithmetic(mu_recv[half, mode, 8:9, :], 8))
             total = row if total is None else total + row
-    courant_buf[...] = jnp.zeros((8, 128), f32)
-    courant_buf[0:1, 0 : 4 * CELLS] = total
+    courant_buf[...] = jnp.broadcast_to(total, (8, 128))
     turn = lax.rem(128 - lax.div(me, 8) * CELLS, 128)
     turned = pltpu.roll(courant_buf[...], turn, 1) * (-1.0 / math.sqrt(K))
     courant_out[...] = turned[0:1, 0:CELLS]
@@ -521,8 +535,8 @@
             pltpu.VMEM((4, 2 * PLANES, 9, WIDTH), jnp.int32),
             pltpu.VMEM((2, 4, 2 * PLANES, 9, WIDTH), jnp.int32),
             pltpu.VMEM((2, NH, CELLS, WIDTH), bf16),
-            pltpu.VMEM((OWNERS, 10, WIDTH), jnp.int32),
-            pltpu.VMEM((2, NH, 10, WIDTH), jnp.int32),
+            pltpu.VMEM((OWNERS, 9, WIDTH), jnp.int32),
+            pltpu.VMEM((2, NH, 9, WIDTH), jnp.int32),
             pltpu.VMEM((OWNERS, 9, WIDTH), jnp.int32),
             pltpu.VMEM((PLANES, CYZ), f32),
             pltpu.VMEM((PLANES, CYZ), jnp.int32),
@@ -547,7 +561,7 @@
             pltpu.SemaphoreType.DMA((2, 9)),
             pltpu.SemaphoreType.DMA((4,)),
             pltpu.SemaphoreType.DMA((4,)),
-            pltpu.SemaphoreType.REGULAR,
+            pltpu.SemaphoreType.REGULAR((3,)),
         ],
         compiler_params=pltpu.CompilerParams(
             collective_id=0, has_side_effects=True, vmem_limit_bytes=60 * 2**20

time: 46.9 us -> 45.7 us (0.974)
  the two profiles are of different devices: /device:TPU:2 before, /device:TPU:32 now
where the time goes in v4:
time: 45.7 us; the launch traced here: 45.5 us
  Pallas kernels  44.8 us (98%)
  between operations  0.64 us (1%)
    pallas_call x1, Pallas kernels, body(): pl.pallas_call(functools.partial(kernel, nodes), out_shape=(jax.ShapeDtyp...  43.3 us
    pallas_call x1, Pallas kernels, body(): pl.pallas_call(finish, out_shape=(jax.ShapeDtypeStruct((rows, WIDTH), f32...  1.57 us

profile of v4, /device:TPU:32, one launch (start us, length us, event | category | flops | bytes accessed | tf_op | source)
XLA Modules:
  0.0 45.5 jit_solution(1728917862354103138)
XLA Ops:
  0.6 43.3 %shard_map.148 = (s32[32,9,128]{2,1,0:T(8,128)}, f32[9,16]{1,0:T(8,128)}, f32[1,16]{1,0:T(1,128)}) custom-call(f32[4,128,128]{2,1,0:T(8,128)} %bitcast.5, bf16[4,128,128]{2,1,0:T(8,128)(2,1)} %bitcast.6, bf16[512,128]{1,0:T(8,128)(2,1)} %src.1, f32[4,128]{1,0:T(4,128)} %bitcast.7, s32[4,128]{1,0:T(4,128)} %bitcast.8, f32[9,16]{1,0:T(8,128)} %strain_hbm.1, ...), custom_call_target="tpu_custom_call" | custom-call | tf_op jit(solution)/shard_map/pallas_call | solution.py:521
  43.9 1.6 %shard_map.149 = (f32[512,128]{1,0:T(8,128)}, f32[9,16]{1,0:T(8,128)}, f32[1,16]{1,0:T(1,128)}) custom-call(s32[32,9,128]{2,1,0:T(8,128)} %get-tuple-element.9.back_hbm, f32[9,16]{1,0:T(8,128)} %get-tuple-element.10.strain_hbm, f32[1,16]{1,0:T(1,128)} %get-tuple-element.11.courant_hbm), custom_call_target="tpu_custom_call" | custom-call | tf_op jit(solution)/shard_map/pallas_call | solution.py:578

commit v5 on v4

--- a/solution.py
+++ b/solution.py
@@ -132,7 +132,7 @@
     src_recv, mu_send, mu_recv, back_send,
     cou, cod, strain,
     outer_ref, inner_ref, inner_t_ref, outer_t_ref, ratio_ref, points_ref, moments_ref,
-    u_buf, es_buf, square_buf, line_buf, column_buf, strain_buf, courant_buf, courant_out,
+    u_buf, es_buf, square_buf, line_buf, column_buf, courant_buf,
     local_sem, halo_send, halo_recv, all_send, all_recv, meet_sem,
 ):
     me = lax.axis_index("coef")
@@ -448,9 +448,7 @@
     courant_buf[...] = jnp.broadcast_to(total, (8, 128))
     turn = lax.rem(128 - lax.div(me, 8) * CELLS, 128)
     turned = pltpu.roll(courant_buf[...], turn, 1) * (-1.0 / math.sqrt(K))
-    courant_out[...] = turned[0:1, 0:CELLS]
-    outs = [pltpu.make_async_copy(courant_out, out_courant, local_sem.at[15])]
-    outs[0].start()
+    out_courant[...] = turned[0:1, 0:CELLS]
 
     wait_all(src_31, all_recv.at[0])
     source = jnp.concatenate(
@@ -474,43 +472,31 @@
             preferred_element_type=f32,
         )
         strain_sum = part if strain_sum is None else strain_sum + part
-    strain_buf[...] = strain_sum[0:9, :]
-    outs.append(pltpu.make_async_copy(strain_buf, out_strain, local_sem.at[16]))
-    outs[1].start()
+    out_strain[...] = strain_sum[0:9, :]
 
     own_back.wait()
-    for copy in outs:
-        copy.wait()
     wait_all(src_31, all_send.at[0])
     wait_all(mu_send.at[pl.ds(0, OWNERS - 1)], all_send.at[1])
     wait_all(back_send.at[pl.ds(0, OWNERS - 1)], all_send.at[3])
     wait_all(back_send.at[pl.ds(0, OWNERS - 1)], all_recv.at[3])
 
 
-def finish(
-    back_hbm, strain_hbm, courant_hbm, out_source, out_strain, out_courant, back, source, sem
-):
-    small = [
-        pltpu.make_async_copy(strain_hbm, out_strain, sem.at[0]),
-        pltpu.make_async_copy(courant_hbm, out_courant, sem.at[1]),
+def finish(back, strain, courant, out_source, out_strain, out_courant, source, sem):
+    stores = [
+        pltpu.make_async_copy(strain, out_strain, sem.at[0]),
+        pltpu.make_async_copy(courant, out_courant, sem.at[1]),
     ]
-    loads = [
-        pltpu.make_async_copy(back_hbm.at[here], back.at[here], sem.at[2 + part])
-        for part, here in enumerate(pl.ds(n * 8, 8) for n in range(4))
-    ]
-    for copy in loads + small:
+    for copy in stores:
         copy.start()
-    stores = []
     for part in range(4):
-        loads[part].wait()
         for n in range(part * 8, part * 8 + 8):
             low, high = decode(back[n, 0:8, :], back[n, 8:9, :], 1.0)
             source[n * CELLS : n * CELLS + 8, :] = low
             source[n * CELLS + 8 : n * CELLS + 16, :] = high
         here = pl.ds(part * 128, 128)
-        stores.append(pltpu.make_async_copy(source.at[here], out_source.at[here], sem.at[6 + part]))
+        stores.append(pltpu.make_async_copy(source.at[here], out_source.at[here], sem.at[2 + part]))
         stores[-1].start()
-    for copy in small + stores:
+    for copy in stores:
         copy.wait()
 
 
@@ -518,6 +504,7 @@
     nodes, *constants = tables()
     rows = PLANES * CYZ
     hbm = pl.BlockSpec(memory_space=pltpu.HBM)
+    vmem = pl.BlockSpec(memory_space=pltpu.VMEM)
     results = pl.pallas_call(
         functools.partial(kernel, nodes),
         out_shape=(
@@ -526,7 +513,7 @@
             jax.ShapeDtypeStruct((1, CELLS), f32),
         ),
         in_specs=[hbm] * 13,
-        out_specs=[hbm] * 3,
+        out_specs=[vmem] * 3,
         scratch_shapes=[
             pltpu.VMEM((PLANES, CYZ, WIDTH), f32),
             pltpu.VMEM((3 * PLANES, CYZ, WIDTH), bf16),
@@ -553,10 +540,8 @@
             pltpu.VMEM((CELLS, POINTS), f32),
             pltpu.VMEM((CELLS, POINTS), f32),
             pltpu.VMEM((128, 128), f32),
-            pltpu.VMEM((9, CELLS), f32),
             pltpu.VMEM((8, WIDTH), f32),
-            pltpu.VMEM((1, CELLS), f32),
-            pltpu.SemaphoreType.DMA((17,)),
+            pltpu.SemaphoreType.DMA((15,)),
             pltpu.SemaphoreType.DMA((2, 9)),
             pltpu.SemaphoreType.DMA((2, 9)),
             pltpu.SemaphoreType.DMA((4,)),
@@ -564,16 +549,21 @@
             pltpu.SemaphoreType.REGULAR((3,)),
         ],
         compiler_params=pltpu.CompilerParams(
-            collective_id=0, has_side_effects=True, vmem_limit_bytes=60 * 2**20
+            collective_id=0, has_side_effects=True, vmem_limit_bytes=30 * 2**20
         ),
     )(
-        cotangent.reshape(PLANES, CYZ, WIDTH),
-        transport_state.reshape(PLANES, CYZ, WIDTH),
-        source_state,
-        courant.reshape(PLANES, CYZ),
-        upwind_codes.reshape(PLANES, CYZ),
-        strain_rate,
-        *[jnp.asarray(table) for table in constants],
+        *[
+            pltpu.with_memory_space_constraint(array, pltpu.HBM)
+            for array in (
+                cotangent.reshape(PLANES, CYZ, WIDTH),
+                transport_state.reshape(PLANES, CYZ, WIDTH),
+                source_state,
+                courant.reshape(PLANES, CYZ),
+                upwind_codes.reshape(PLANES, CYZ),
+                strain_rate,
+                *[jnp.asarray(table) for table in constants],
+            )
+        ],
     )
     adj_source, adj_strain, adj_courant = pl.pallas_call(
         finish,
@@ -582,14 +572,13 @@
             jax.ShapeDtypeStruct((9, CELLS), f32),
             jax.ShapeDtypeStruct((1, CELLS), f32),
         ),
-        in_specs=[hbm] * 3,
+        in_specs=[vmem] * 3,
         out_specs=[hbm] * 3,
         scratch_shapes=[
-            pltpu.VMEM((OWNERS, 9, WIDTH), jnp.int32),
             pltpu.VMEM((rows, WIDTH), f32),
-            pltpu.SemaphoreType.DMA((10,)),
+            pltpu.SemaphoreType.DMA((6,)),
         ],
-        compiler_params=pltpu.CompilerParams(vmem_limit_bytes=60 * 2**20),
+        compiler_params=pltpu.CompilerParams(vmem_limit_bytes=8 * 2**20),
     )(*results)
     return adj_source, adj_strain, adj_courant.reshape(CELLS)
 

time: 45.7 us -> 44.7 us (0.978)
  Pallas kernels: 44.8 us -> 43.9 us
    pallas_call x1, Pallas kernels: 1.57 us -> 0.77 us  [body(): pl.pallas_call(finish, out_shape=(jax.ShapeDtypeStruct((rows, WIDTH), f32...]
where the time goes in v5:
time: 44.7 us; the launch traced here: 44.6 us
  Pallas kernels  43.9 us (98%)
  between operations  0.64 us (1%)
    pallas_call x1, Pallas kernels, body(): pl.pallas_call(functools.partial(kernel, nodes), out_shape=(jax.ShapeDtyp...  43.1 us

profile of v5, /device:TPU:32, one launch (start us, length us, event | category | flops | bytes accessed | tf_op | source)
XLA Modules:
  0.0 44.6 jit_solution(4219429489492828785)
XLA Ops:
  0.6 43.1 %shard_map.148 = (s32[32,9,128]{2,1,0:T(8,128)S(1)}, f32[9,16]{1,0:T(8,128)S(1)}, f32[1,16]{1,0:T(1,128)S(1)}) custom-call(f32[4,128,128]{2,1,0:T(8,128)} %bitcast.5, bf16[4,128,128]{2,1,0:T(8,128)(2,1)} %bitcast.6, bf16[512,128]{1,0:T(8,128)(2,1)} %src.1, f32[4,128]{1,0:T(4,128)} %bitcast.7, s32[4,128]{1,0:T(4,128)} %bitcast.8, f32[9,16]{1,0:T(8,128)} %strain_hbm.1, ...), custom_call_target="tpu_custom_call" | custom-call | tf_op jit(solution)/shard_map/pallas_call | solution.py:508
  43.8 0.8 %shard_map.149 = (f32[512,128]{1,0:T(8,128)}, f32[9,16]{1,0:T(8,128)}, f32[1,16]{1,0:T(1,128)}) custom-call(s32[32,9,128]{2,1,0:T(8,128)S(1)} %get-tuple-element.9.back, f32[9,16]{1,0:T(8,128)S(1)} %get-tuple-element.10.strain, f32[1,16]{1,0:T(1,128)S(1)} %get-tuple-element.11.courant), custom_call_target="tpu_custom_call" | custom-call | tf_op jit(solution)/shard_map/pallas_call | solution.py:568

commit v6 on v5

--- a/solution.py
+++ b/solution.py
@@ -188,11 +188,11 @@
         if kind == 0:
             source, dest, sem = scbuf.at[1], scbuf.at[place], 0
         elif kind == 1:
-            rows = pl.ds(pl.multiple_of(part * 32, 32), 32)
+            rows = pl.ds(pl.multiple_of(part * 16, 16), 16)
             planes = pl.ds(place * PLANES, PLANES)
             source, dest, sem = tst.at[:, rows], tbuf.at[planes, rows], 1 + part
         else:
-            source, dest, sem = code_send.at[part], code_recv.at[way, part], 5 + part
+            source, dest, sem = code_send.at[part], code_recv.at[way, part], 9 + part
         return pltpu.make_async_remote_copy(
             src_ref=source,
             dst_ref=dest,
@@ -202,26 +202,25 @@
             device_id_type=MESH,
         )
 
-    first_part = lax.div(lax.rem(me, 8), 2)
-    order = [lax.rem(first_part + n, 4) for n in (0, 1, 3, 2)]
+    first_part = lax.rem(me, 8)
+    order = [lax.rem(first_part + n, 8) for n in range(8)]
     for way in range(2):
         halo_copy(way, 0, 0).start()
     for way in range(2):
         halo_copy(way, 1, order[0]).start()
     loads[0].wait()
-    for step in range(4):
+    for step in range(8):
         for p in range(PLANES):
-            for n in range(2):
-                y = order[step] * 32 + n * 16
-                word, level = encode(
-                    gbuf[p, pl.ds(pl.multiple_of(y, 8), 8), :],
-                    gbuf[p, pl.ds(pl.multiple_of(y + 8, 8), 8), :],
-                )
-                code_send[order[step], p * 2 + n, 0:8, :] = word
-                code_send[order[step], p * 2 + n, 8:9, :] = level
+            y = order[step] * 16
+            word, level = encode(
+                gbuf[p, pl.ds(pl.multiple_of(y, 8), 8), :],
+                gbuf[p, pl.ds(pl.multiple_of(y + 8, 8), 8), :],
+            )
+            code_send[order[step], p, 0:8, :] = word
+            code_send[order[step], p, 8:9, :] = level
         for way in range(2):
             halo_copy(way, 2, order[step]).start()
-        if step < 3:
+        if step < 7:
             for way in range(2):
                 halo_copy(way, 1, order[step + 1]).start()
     for n in (6, 2, 3, 4, 5, 10, 12):
@@ -265,11 +264,10 @@
     sct_buf[...] = jnp.transpose(signed)
     ones = jnp.ones((8, WIDTH), bf16)
 
-    def chunk(quarter, n):
-        part = quarter * 2 + n
+    def chunk(part):
         mu_parts, acc_parts = [], []
         coded = [
-            (code_recv.at[way, quarter, p * 2 + n], way * 8 + p)
+            (code_recv.at[way, part, p], way * 8 + p)
             for way in range(2)
             for p in range(PLANES)
         ]
@@ -330,19 +328,15 @@
             mu_send[dest, 8:9, :] = jnp.bitwise_or(codes, level + 200)
 
     def chunks(step, _):
-        part = lax.rem(first_part + step + lax.div(step, 2) * (5 - 2 * step), 4)
+        part = lax.rem(first_part + step, 8)
         for kind in (1, 2):
             for way in range(2):
                 halo_copy(way, kind, part).wait()
 
-        def half(n, _):
-            chunk(part, n)
-            return 0
-
-        lax.fori_loop(0, 2, half, 0)
+        chunk(part)
         return 0
 
-    lax.fori_loop(0, 4, chunks, 0)
+    lax.fori_loop(0, 8, chunks, 0)
 
     pl.semaphore_wait(meet_sem.at[2], 2)
     for away, other in far + near:
@@ -519,8 +513,8 @@
             pltpu.VMEM((3 * PLANES, CYZ, WIDTH), bf16),
             pltpu.VMEM((3, PLANES, CYZ), f32),
             pltpu.VMEM((128, 128), f32),
-            pltpu.VMEM((4, 2 * PLANES, 9, WIDTH), jnp.int32),
-            pltpu.VMEM((2, 4, 2 * PLANES, 9, WIDTH), jnp.int32),
+            pltpu.VMEM((8, PLANES, 9, WIDTH), jnp.int32),
+            pltpu.VMEM((2, 8, PLANES, 9, WIDTH), jnp.int32),
             pltpu.VMEM((2, NH, CELLS, WIDTH), bf16),
             pltpu.VMEM((OWNERS, 9, WIDTH), jnp.int32),
             pltpu.VMEM((2, NH, 9, WIDTH), jnp.int32),
@@ -542,8 +536,8 @@
             pltpu.VMEM((128, 128), f32),
             pltpu.VMEM((8, WIDTH), f32),
             pltpu.SemaphoreType.DMA((15,)),
-            pltpu.SemaphoreType.DMA((2, 9)),
-            pltpu.SemaphoreType.DMA((2, 9)),
+            pltpu.SemaphoreType.DMA((2, 17)),
+            pltpu.SemaphoreType.DMA((2, 17)),
             pltpu.SemaphoreType.DMA((4,)),
             pltpu.SemaphoreType.DMA((4,)),
             pltpu.SemaphoreType.REGULAR((3,)),

time: 44.7 us -> 44.9 us (level)
  the two profiles are of different devices: /device:TPU:32 before, /device:TPU:48 now
where the time goes in v6:
time: 44.9 us; the launch traced here: 44.8 us
  Pallas kernels  44.1 us (98%)
  between operations  0.64 us (1%)
    pallas_call x1, Pallas kernels, body(): pl.pallas_call(functools.partial(kernel, nodes), out_shape=(jax.ShapeDtyp...  43.3 us

profile of v6, /device:TPU:48, one launch (start us, length us, event | category | flops | bytes accessed | tf_op | source)
XLA Modules:
  0.0 44.8 jit_solution(9410107388234537100)
XLA Ops:
  0.6 43.3 %shard_map.148 = (s32[32,9,128]{2,1,0:T(8,128)S(1)}, f32[9,16]{1,0:T(8,128)S(1)}, f32[1,16]{1,0:T(1,128)S(1)}) custom-call(f32[4,128,128]{2,1,0:T(8,128)} %bitcast.5, bf16[4,128,128]{2,1,0:T(8,128)(2,1)} %bitcast.6, bf16[512,128]{1,0:T(8,128)(2,1)} %src.1, f32[4,128]{1,0:T(4,128)} %bitcast.7, s32[4,128]{1,0:T(4,128)} %bitcast.8, f32[9,16]{1,0:T(8,128)} %strain_hbm.1, ...), custom_call_target="tpu_custom_call" | custom-call | tf_op jit(solution)/shard_map/pallas_call | solution.py:502
  44.0 0.8 %shard_map.149 = (f32[512,128]{1,0:T(8,128)}, f32[9,16]{1,0:T(8,128)}, f32[1,16]{1,0:T(1,128)}) custom-call(s32[32,9,128]{2,1,0:T(8,128)S(1)} %get-tuple-element.9.back, f32[9,16]{1,0:T(8,128)S(1)} %get-tuple-element.10.strain, f32[1,16]{1,0:T(1,128)S(1)} %get-tuple-element.11.courant), custom_call_target="tpu_custom_call" | custom-call | tf_op jit(solution)/shard_map/pallas_call | solution.py:562
